TPU v7x, 32 devices: a whole 2x2x4 slice. The times are simulated.
32 devices in a mesh: seq: 16 (over z, y, x), tp: 2 (over core).
Axes of the slice: x: 2, y: 2, z: 4, core: 2. Of those that a mesh axis runs over, the one named last changes fastest.
Arguments:
- layer_input: bfloat16 [4096, 768], P('seq'), may hold values from -6 to 6
- mixer_gain: float32 [768], replicated, may hold values from 0.1 to 1.9
- in_proj: bfloat16 [192, 3, 768], replicated, may hold values from -0.4375 to 0.4375
- short_taps: float32 [3, 3, 768], replicated, may hold values from -3 to 3
- filter_w1: float32 [5, 128], replicated, may hold values from -2.5 to 2.5
- filter_b1: float32 [128], replicated, may hold values from -3.140625 to 3.140625
- filter_w2: float32 [128, 128], replicated, may hold values from -0.5 to 0.5
- filter_w3: float32 [128, 768], P(None, 'seq'), may hold values from -0.015625 to 0.015625
- filter_decay: float32 [768], P('seq'), may hold values from 0.5 to 128
- out_proj: bfloat16 [192, 768], replicated, may hold values from -0.4375 to 0.4375
- glu_gain: float32 [768], replicated, may hold values from 0.1 to 1.9
- glu_in: bfloat16 [4, 192, 2, 768], P(None, None, None, 'tp'), may hold values from -0.4375 to 0.4375
- glu_out: bfloat16 [768, 768], P('tp'), may hold values from -0.21875 to 0.21875
- out_grad: bfloat16 [4096, 768], P(('seq', 'tp')), may hold values from -6 to 6
Outputs:
- layer_output: bfloat16 [4096, 768], P(('seq', 'tp'))
- input_grad: bfloat16 [4096, 768], P('seq')
- mixer_gain_grad: float32 [768], replicated
- in_proj_grad: float32 [192, 3, 768], replicated
- short_taps_grad: float32 [3, 3, 768], replicated
- filter_w1_grad: float32 [5, 128], replicated
- filter_b1_grad: float32 [128], replicated
- filter_w2_grad: float32 [128, 128], replicated
- filter_w3_grad: float32 [128, 768], P(None, 'seq')
- out_proj_grad: float32 [192, 768], replicated
- glu_gain_grad: float32 [768], replicated
- glu_in_grad: float32 [4, 192, 2, 768], P(None, None, None, 'tp')
- glu_out_grad: float32 [768, 768], P('tp')
All inputs are finite; a program needn't handle non-finite values.
Results may differ from a plain program's by a relative error of at most 0.012.
Values may be sent and summed in bfloat16 or wider, within the bound.
No kernel may reach another device: no remote copies, remote signals or barrier semaphores. Data moves between devices by JAX's collectives and lax.ppermute only.
A program may use at most 128 MiB of HBM per device.

v0:
```python
import math

import jax
import jax.numpy as jnp
from jax import lax
from jax.sharding import PartitionSpec as P

EMB = 5
MIN_LEN = 8192


EXACT_PRODUCT = lax.Precision.HIGHEST
EPSILON = 1e-05


def shifted(array, axis, by):
    devices = lax.axis_size(axis)
    pairs = [(i, i + by) for i in range(devices) if 0 <= i + by < devices]
    return lax.ppermute(array, axis, pairs)


def layer_normed(values, gain):
    centered = values - jnp.mean(values, axis=-1, keepdims=True)
    variance = jnp.mean(centered * centered, axis=-1, keepdims=True)
    return centered * lax.rsqrt(variance + EPSILON) * gain


def gated_units(gate_part, up_part):
    return jax.nn.gelu(gate_part, approximate=False) * up_part


def filter_taps(weight_first, bias_first, weight_second, weight_third, decay_rates, seq_length):
    period = 2 * seq_length
    step_index = jnp.arange(period, dtype=jnp.int32)
    lag_steps = jnp.where(step_index < seq_length, step_index, step_index - period).astype(
        jnp.float32
    )
    position = lag_steps / seq_length
    columns = [position]
    band_count = (EMB - 1) // 2
    for band_index in range(1, band_count + 1):
        columns.append(jnp.cos(2.0 * math.pi * band_index * position))
    for band_index in range(1, band_count + 1):
        columns.append(jnp.sin(2.0 * math.pi * band_index * position))
    features = jnp.stack(columns, axis=1)
    hidden_first = jnp.sin(jnp.dot(features, weight_first, precision=EXACT_PRODUCT) + bias_first)
    hidden_second = jnp.sin(jnp.dot(hidden_first, weight_second, precision=EXACT_PRODUCT))
    shaped = jnp.dot(hidden_second, weight_third, precision=EXACT_PRODUCT)
    return shaped * jnp.exp(-jnp.abs(lag_steps)[:, None] * decay_rates[None, :] / seq_length)


def radix_split(period):
    exponent = period.bit_length() - 1
    first_radix = 2 ** (exponent // 2)
    return (first_radix, period // first_radix)


def angle_table(row_count, col_count, modulus):
    row_ids = jnp.arange(row_count, dtype=jnp.int32)[:, None]
    col_ids = jnp.arange(col_count, dtype=jnp.int32)[None, :]
    return 2.0 * math.pi / modulus * (row_ids * col_ids % modulus).astype(jnp.float32)


def dft_tables(period):
    first_radix, second_radix = radix_split(period)
    first_angle = angle_table(first_radix, first_radix, first_radix)
    twist_angle = angle_table(first_radix, second_radix, period)
    second_angle = angle_table(second_radix, second_radix, second_radix)
    return (
        jnp.cos(first_angle),
        jnp.sin(first_angle),
        jnp.cos(twist_angle),
        jnp.sin(twist_angle),
        jnp.cos(second_angle),
        jnp.sin(second_angle),
    )


def forward_dft(signal, tables):
    first_cos, first_sin, twist_cos, twist_sin, second_cos, second_sin = tables
    used_rows = signal.shape[1]
    section_real = jnp.einsum(
        "kn,bnm->bkm", first_cos[:, :used_rows], signal, precision=EXACT_PRODUCT
    )
    section_imag = -jnp.einsum(
        "kn,bnm->bkm", first_sin[:, :used_rows], signal, precision=EXACT_PRODUCT
    )
    twisted_real = section_real * twist_cos + section_imag * twist_sin
    twisted_imag = section_imag * twist_cos - section_real * twist_sin
    spec_real = jnp.einsum(
        "bkm,mq->bkq", twisted_real, second_cos, precision=EXACT_PRODUCT
    ) + jnp.einsum("bkm,mq->bkq", twisted_imag, second_sin, precision=EXACT_PRODUCT)
    spec_imag = jnp.einsum(
        "bkm,mq->bkq", twisted_imag, second_cos, precision=EXACT_PRODUCT
    ) - jnp.einsum("bkm,mq->bkq", twisted_real, second_sin, precision=EXACT_PRODUCT)
    return (spec_real, spec_imag)


def inverse_dft(spec_real, spec_imag, tables, kept_rows):
    first_cos, first_sin, twist_cos, twist_sin, second_cos, second_sin = tables
    period = first_cos.shape[0] * second_cos.shape[0]
    back_real = jnp.einsum(
        "bkq,mq->bkm", spec_real, second_cos, precision=EXACT_PRODUCT
    ) - jnp.einsum("bkq,mq->bkm", spec_imag, second_sin, precision=EXACT_PRODUCT)
    back_imag = jnp.einsum(
        "bkq,mq->bkm", spec_imag, second_cos, precision=EXACT_PRODUCT
    ) + jnp.einsum("bkq,mq->bkm", spec_real, second_sin, precision=EXACT_PRODUCT)
    turned_real = back_real * twist_cos - back_imag * twist_sin
    turned_imag = back_imag * twist_cos + back_real * twist_sin
    result = jnp.einsum(
        "kn,bkm->bnm", first_cos[:, :kept_rows], turned_real, precision=EXACT_PRODUCT
    ) - jnp.einsum("kn,bkm->bnm", first_sin[:, :kept_rows], turned_imag, precision=EXACT_PRODUCT)
    return result / period


def spectral_product(left_real, left_imag, right_real, right_imag, conjugate):
    if conjugate:
        right_imag = -right_imag
    return (
        left_real * right_real - left_imag * right_imag,
        left_real * right_imag + left_imag * right_real,
    )


def local(
    layer_input,
    mixer_gain,
    in_proj,
    short_taps,
    filter_w1,
    filter_b1,
    filter_w2,
    filter_w3,
    filter_decay,
    out_proj,
    glu_gain,
    glu_in,
    glu_out,
    out_grad,
):
    tok_rows, model_width = layer_input.shape
    block_width = in_proj.shape[0]
    blocks = model_width // block_width
    hidden_local = glu_out.shape[0]
    seq_devices = lax.axis_size("seq")
    tp_devices = lax.axis_size("tp")
    seq_length = min(MIN_LEN, tok_rows * seq_devices)
    seq_index = lax.axis_index("seq")
    tp_index = lax.axis_index("tp")
    half_rows = tok_rows // tp_devices
    at_start = seq_index * tok_rows % seq_length == 0
    at_end = (seq_index + 1) * tok_rows % seq_length == 0
    tables = dft_tables(2 * seq_length)
    first_radix, second_radix = radix_split(2 * seq_length)
    in_weights = in_proj.reshape(block_width, 3, blocks, block_width)
    out_weights = out_proj.reshape(block_width, blocks, block_width)
    down_weights = glu_out.reshape(hidden_local, blocks, block_width)

    def local_filter(weight_first, bias_first, weight_second, weight_third):
        return filter_taps(
            weight_first, bias_first, weight_second, weight_third, filter_decay, seq_length
        ).T

    lag_filter, filter_pull = jax.vjp(local_filter, filter_w1, filter_b1, filter_w2, filter_w3)
    channels = lag_filter.shape[0]
    filter_real, filter_imag = forward_dft(
        lag_filter.reshape(channels, first_radix, second_radix), tables
    )
    input_rows = layer_input.astype(jnp.float32)
    normed_value, first_pull = jax.vjp(layer_normed, input_rows, mixer_gain)
    normed_one = normed_value.astype(jnp.bfloat16)
    normed_one_blocks = normed_one.reshape(tok_rows, blocks, block_width)
    projected = jnp.einsum(
        "tbi,isbo->sbot", normed_one_blocks, in_weights, preferred_element_type=jnp.float32
    )
    projected = projected.reshape(3, model_width, tok_rows).astype(jnp.bfloat16)
    previous = shifted(projected[:, :, tok_rows - 2 :], "seq", 1)
    previous = jnp.where(at_start, jnp.zeros_like(previous), previous)
    extended = jnp.concatenate([previous, projected], axis=2).astype(jnp.float32)
    tap_zero = short_taps[0][:, :, None]
    tap_one = short_taps[1][:, :, None]
    tap_two = short_taps[2][:, :, None]
    short_mixed = (
        tap_zero * extended[:, :, 2:]
        + tap_one * extended[:, :, 1:-1]
        + tap_two * extended[:, :, :-2]
    )
    conv_rows = (short_mixed[0] * short_mixed[1]).astype(jnp.bfloat16)
    conv_channels = lax.all_to_all(conv_rows, "seq", split_axis=0, concat_axis=1, tiled=True)
    total_tokens = conv_channels.shape[1]
    seq_count = total_tokens // seq_length
    signal_shape = (channels * seq_count, first_radix // 2, second_radix)
    spec_grid = (channels, seq_count, first_radix, second_radix)
    flat_grid = (channels * seq_count, first_radix, second_radix)
    signal_real, signal_imag = forward_dft(
        conv_channels.astype(jnp.float32).reshape(signal_shape), tables
    )
    product_real, product_imag = spectral_product(
        signal_real.reshape(spec_grid),
        signal_imag.reshape(spec_grid),
        filter_real[:, None],
        filter_imag[:, None],
        False,
    )
    convolved = inverse_dft(
        product_real.reshape(flat_grid), product_imag.reshape(flat_grid), tables, first_radix // 2
    )
    conv_low = convolved.reshape(channels, total_tokens).astype(jnp.bfloat16)
    conv_back = lax.all_to_all(conv_low, "seq", split_axis=1, concat_axis=0, tiled=True)
    conv_out = conv_back.astype(jnp.float32)
    gated_rows = (short_mixed[2] * conv_out).astype(jnp.bfloat16)
    gated_blocks = gated_rows.reshape(blocks, block_width, tok_rows)
    branch = jnp.einsum(
        "bit,ibo->tbo", gated_blocks, out_weights, preferred_element_type=jnp.float32
    ).reshape(tok_rows, model_width)
    middle = input_rows + branch
    middle_half = lax.dynamic_slice_in_dim(middle, tp_index * half_rows, half_rows, 0)
    normed_half, second_pull = jax.vjp(layer_normed, middle_half, glu_gain)
    normed_two = lax.all_gather(normed_half.astype(jnp.bfloat16), "tp", axis=0, tiled=True)
    normed_blocks = normed_two.reshape(tok_rows, blocks, block_width)
    gate_up = jnp.einsum(
        "tbi,bisf->tsbf", normed_blocks, glu_in, preferred_element_type=jnp.float32
    )
    hidden_value, unit_pull = jax.vjp(gated_units, gate_up[:, 0], gate_up[:, 1])
    hidden = hidden_value.astype(jnp.bfloat16)
    down_sum = lax.psum_scatter(
        jnp.einsum(
            "tbf,fbo->tbo", hidden, down_weights, preferred_element_type=jnp.float32
        ).reshape(lax.axis_size("tp") * half_rows, model_width),
        "tp",
        scatter_dimension=0,
        tiled=True,
    )
    layer_output = (middle_half + down_sum).astype(jnp.bfloat16)
    grad_rows = lax.all_gather(out_grad, "tp", axis=0, tiled=True)
    grad_blocks = grad_rows.reshape(tok_rows, blocks, block_width)
    glu_out_grad = jnp.einsum(
        "tbf,tbo->fbo", hidden, grad_blocks, preferred_element_type=jnp.float32
    ).reshape(hidden_local, model_width)
    hidden_grad = jnp.einsum(
        "tbo,fbo->tbf", grad_blocks, down_weights, preferred_element_type=jnp.float32
    )
    gate_grad, up_grad = unit_pull(hidden_grad)
    gate_up_grad = jnp.stack([gate_grad, up_grad], axis=1).astype(jnp.bfloat16)
    glu_in_grad = jnp.einsum(
        "tbi,tsbf->bisf", normed_blocks, gate_up_grad, preferred_element_type=jnp.float32
    )
    normed_grad = lax.psum_scatter(
        jnp.einsum(
            "tsbf,bisf->tbi", gate_up_grad, glu_in, preferred_element_type=jnp.float32
        ).reshape(lax.axis_size("tp") * half_rows, model_width),
        "tp",
        scatter_dimension=0,
        tiled=True,
    )
    middle_part, gain_part = second_pull(normed_grad)
    middle_half_grad = out_grad.astype(jnp.float32) + middle_part
    middle_grad, gain_parts = (
        lax.all_gather(middle_half_grad, "tp", axis=0, tiled=True),
        lax.all_gather(gain_part[None, :], "tp", axis=0, tiled=True),
    )
    glu_gain_grad = jnp.sum(gain_parts, axis=0)
    branch_grad = middle_grad.astype(jnp.bfloat16)
    branch_blocks = branch_grad.reshape(tok_rows, blocks, block_width)
    out_proj_grad = jnp.einsum(
        "bit,tbo->ibo", gated_blocks, branch_blocks, preferred_element_type=jnp.float32
    ).reshape(block_width, model_width)
    gated_grad = jnp.einsum(
        "tbo,ibo->bit", branch_blocks, out_weights, preferred_element_type=jnp.float32
    ).reshape(model_width, tok_rows)
    third_grad = gated_grad * conv_out
    conv_grad = (gated_grad * short_mixed[2]).astype(jnp.bfloat16)
    conv_grad_channels = lax.all_to_all(conv_grad, "seq", split_axis=0, concat_axis=1, tiled=True)
    grad_real, grad_imag = forward_dft(
        conv_grad_channels.astype(jnp.float32).reshape(signal_shape), tables
    )
    again_channels = lax.all_to_all(conv_rows, "seq", split_axis=0, concat_axis=1, tiled=True)
    saved_real, saved_imag = forward_dft(
        again_channels.astype(jnp.float32).reshape(signal_shape), tables
    )
    back_real, back_imag = spectral_product(
        grad_real.reshape(spec_grid),
        grad_imag.reshape(spec_grid),
        filter_real[:, None],
        filter_imag[:, None],
        True,
    )
    input_conv_grad = inverse_dft(
        back_real.reshape(flat_grid), back_imag.reshape(flat_grid), tables, first_radix // 2
    )
    cross_real, cross_imag = spectral_product(
        grad_real.reshape(spec_grid),
        grad_imag.reshape(spec_grid),
        saved_real.reshape(spec_grid),
        saved_imag.reshape(spec_grid),
        True,
    )
    filter_grad = inverse_dft(
        jnp.sum(cross_real, axis=1), jnp.sum(cross_imag, axis=1), tables, first_radix
    ).reshape(channels, 2 * seq_length)
    grad_back = lax.all_to_all(
        input_conv_grad.reshape(channels, total_tokens).astype(jnp.bfloat16),
        "seq",
        split_axis=1,
        concat_axis=0,
        tiled=True,
    ).astype(jnp.float32)
    short_grad = jnp.stack([grad_back * short_mixed[1], grad_back * short_mixed[0], third_grad])
    short_taps_grad = jnp.stack(
        [
            jnp.sum(short_grad * extended[:, :, 2:], axis=2),
            jnp.sum(short_grad * extended[:, :, 1:-1], axis=2),
            jnp.sum(short_grad * extended[:, :, :-2], axis=2),
        ]
    )
    following = shifted(short_grad[:, :, :2], "seq", -1)
    following = jnp.where(at_end, jnp.zeros_like(following), following)
    grad_extended = jnp.concatenate([short_grad, following], axis=2)
    projected_grad = (
        tap_zero * grad_extended[:, :, :tok_rows]
        + tap_one * grad_extended[:, :, 1 : tok_rows + 1]
        + tap_two * grad_extended[:, :, 2:]
    )
    projected_blocks = projected_grad.astype(jnp.bfloat16).reshape(3, blocks, block_width, tok_rows)
    in_proj_grad = jnp.einsum(
        "tbi,sbot->isbo", normed_one_blocks, projected_blocks, preferred_element_type=jnp.float32
    ).reshape(block_width, 3, model_width)
    normed_one_grad = jnp.einsum(
        "sbot,isbo->tbi", projected_blocks, in_weights, preferred_element_type=jnp.float32
    ).reshape(tok_rows, model_width)
    input_part, mixer_gain_grad = first_pull(normed_one_grad)
    input_grad = (middle_grad + input_part).astype(jnp.bfloat16)
    weight_first_grad, bias_first_grad, weight_second_grad, filter_w3_grad = filter_pull(
        filter_grad
    )
    summed = lax.psum(
        (
            mixer_gain_grad,
            in_proj_grad,
            short_taps_grad,
            weight_first_grad,
            bias_first_grad,
            weight_second_grad,
            out_proj_grad,
            glu_gain_grad,
            glu_in_grad,
            glu_out_grad,
        ),
        "seq",
    )
    mixer_totals = list(summed[:8])
    glu_in_total = summed[8]
    glu_out_total = summed[9]
    return (
        layer_output,
        input_grad,
        mixer_totals[0],
        mixer_totals[1],
        mixer_totals[2],
        mixer_totals[3],
        mixer_totals[4],
        mixer_totals[5],
        filter_w3_grad,
        mixer_totals[6],
        mixer_totals[7],
        glu_in_total,
        glu_out_total,
    )


def solution(mesh):
    placed = (
        P("seq", None),
        P(),
        P(),
        P(),
        P(),
        P(),
        P(),
        P(None, "seq"),
        P("seq"),
        P(),
        P(),
        P(None, None, None, "tp"),
        P("tp", None),
        P(("seq", "tp"), None),
    )
    return jax.shard_map(
        local,
        mesh=mesh,
        in_specs=placed,
        out_specs=(
            P(("seq", "tp"), None),
            P("seq", None),
            P(),
            P(),
            P(),
            P(),
            P(),
            P(),
            P(None, "seq"),
            P(),
            P(),
            P(None, None, None, "tp"),
            P("tp", None),
        ),
        check_vma=False,
    )
```

profile of v0, /device:TPU:0, one launch (start us, length us, event | category | flops | bytes accessed | tf_op | source)
XLA Modules:
  0.0 530.6 jit_solution(16521991954178008103)
XLA Ops:
  9.3 2.9 reshape.357
  14.9 4.8 collective-permute-start
  22.3 22.7 %fusion.353 = (f32[8192,128]{1,0:T(8,128)S(1)}, f32[8192,128]{1,0:T(8,128)}) fusion(f32[128]{0:T(128)S(1)} %copy-done.93, f32[8192,5]{0,1:T(8,128)S(1)} %stack.38, f32[5,128]{1,0:T(8,128)S(1)} %copy-done.92), kind=kOutput, calls=%fused_computation.411 | convolution fusion | flops 63963136 | bytes 8555520 | tf_op jit(solution)/shard_map/jvp()/dot_general | solution.py:46
  45.0 19.8 %fusion.354 = (f32[8192,128]{1,0:T(8,128)S(1)}, f32[8192,128]{1,0:T(8,128)}) fusion(f32[8192,128]{1,0:T(8,128)S(1)} %get-tuple-element.106, f32[128,128]{1,0:T(8,128)S(1)} %copy-done.66), kind=kOutput, calls=%fused_computation.412 | convolution fusion | flops 1610612736 | bytes 12648448 | tf_op jit(solution)/shard_map/jvp()/dot_general | solution.py:47
  64.8 4.6 fusion.60
  73.0 1.7 fusion.124
  74.8 2.9 convolution_subtract_fusion.4
  79.0 2.2 maximum_convert_fusion
  81.2 2.4 multiply_add_fusion
  85.4 6.4 %all-to-all-start = ((bf16[16,48,256]{2,1,0:T(8,128)(2,1)}), bf16[16,48,256]{2,1,0:T(8,128)(2,1)}, u32[]{:S(2)}, u32[]{:S(2)}) async-start(bf16[16,48,256]{2,1,0:T(8,128)(2,1)} %bitcast.465), calls=%async_computation | async-start | bytes 786432 | tf_op jit(solution)/shard_map/all_to_all | solution.py:189
  91.9 3.2 fusion.128
  95.2 2.9 convolution_add_fusion.5
  98.1 5.7 %all-to-all-done = bf16[16,48,256]{2,1,0:T(8,128)(2,1)} async-done(((bf16[16,48,256]{2,1,0:T(8,128)(2,1)}), bf16[16,48,256]{2,1,0:T(8,128)(2,1)}, u32[]{:S(2)}, u32[]{:S(2)}) %all-to-all-start) | async-done | bytes 393248 | tf_op jit(solution)/shard_map/all_to_all | solution.py:189
  111.9 3.3 multiply_add_fusion.3
  115.1 1.7 fusion.166
  116.8 1.7 fusion.168
  118.5 1.7 convolution_add_fusion.4
  120.3 1.7 convolution_subtract_fusion.3
  123.2 2.0 fusion.81
  127.2 4.3 all-to-all-start.1
  132.5 2.1 reshape.360
  134.6 2.2 all_gather.13
  138.0 2.3 copy.134
  140.3 2.7 fusion.357
  146.5 2.1 all_gather.12
  150.1 3.8 fusion.117
  156.8 2.7 fusion.356
  159.6 1.7 copy.135
  162.7 2.8 copy.151
  167.6 1.9 multiply_reduce_fusion.5
  169.5 8.6 %reduce-scatter.3.cloned.1.call-done = f32[128,768]{0,1:T(8,128)} async-done(((f32[256,768]{0,1:T(8,128)}), f32[128,768]{0,1:T(8,128)}) %reduce-scatter.3.cloned.1.call-update) | async-done | bytes 393232 | tf_op jit(solution)/shard_map/reduce_scatter | solution.py:226
  178.1 1.8 add_add_fusion.2
  180.0 2.5 all_gather.14
  185.4 7.2 %all-to-all-start.2 = ((bf16[16,48,256]{2,1,0:T(8,128)(2,1)}), bf16[16,48,256]{2,1,0:T(8,128)(2,1)}, u32[]{:S(2)}, u32[]{:S(2)}) async-start(bf16[16,48,256]{2,1,0:T(8,128)(2,1)} %multiply_convert_fusion.1), calls=%async_computation.4 | async-start | bytes 786432 | tf_op jit(solution)/shard_map/all_to_all | solution.py:273
  192.6 3.3 fusion.20
  197.2 2.2 copy.149
  199.4 2.0 bitcast_multiply_fusion.18
  201.4 4.0 all-to-all-done.2
  208.3 1.7 fusion.130
  210.1 1.7 fusion.134
  211.8 1.7 convolution_add_fusion.3
  214.1 2.5 multiply_add_fusion.1
  216.6 1.7 fusion.156
  218.3 1.9 fusion.158
  221.9 2.8 convolution_subtract_fusion
  226.4 1.7 fusion.160
  228.1 1.7 convolution_subtract_fusion.1
  235.1 3.6 all-to-all-start.3
  238.8 3.4 fusion.22
  242.3 2.0 subtract_multiply_fusion
  245.5 21.7 %convolution_multiply_fusion.1 = f32[8192,128]{1,0:T(8,128)} fusion(f32[128,48]{0,1:T(8,128)S(1)} %copy-done.73, f32[8192,128]{1,0:T(8,128)S(1)} %copy-done.9, f32[6,8,64,128]{3,2,1,0:T(8,128)S(1)} %bitcast.441, f32[48]{0:T(128)S(1)} %copy-done.89, f32[8192]{0:T(1024)S(1)} %copy-done.61), kind=kOutput, calls=%fused_computation.1 | convolution fusion | flops 606208000 | bytes 10019008 | tf_op jit(solution)/shard_map/transpose(jvp())/dot_general | solution.py:48
  271.7 1.7 collective-permute-start.1
  273.4 10.8 %fusion.359 = f32[128,128]{1,0:T(8,128)} fusion(f32[8192,128]{1,0:T(8,128)} %copy-done.6, f32[8192,128]{1,0:T(8,128)} %convolution_multiply_fusion.1), kind=kOutput, calls=%fused_computation.417 | convolution fusion | flops 1610612736 | bytes 8454144 | tf_op jit(solution)/shard_map/transpose(jvp())/dot_general | solution.py:47
  288.0 4.9 multiply_reduce_fusion.2
  294.0 1.9 convolution_bitcast_fusion.2
  295.9 4.4 copy.148
  300.3 3.7 reshape.373
  305.7 1.9 all-gather.1
  307.7 20.5 %fusion.355 = (f32[128]{0:T(128)S(1)}, f32[8192,128]{1,0:T(8,128)S(1)}) fusion(f32[8192,128]{1,0:T(8,128)} %get-tuple-element.107, f32[8192,128]{1,0:T(8,128)} %convolution_multiply_fusion.1, f32[128,128]{1,0:T(8,128)S(1)} %copy-done.67), kind=kOutput, calls=%fused_computation.413 | convolution fusion | flops 1612709760 | bytes 12648960 | tf_op jit(solution)/shard_map/transpose(jvp())/dot_general | solution.py:47
  328.2 2.1 fusion.358
  330.5 4.1 fusion.94
  337.6 81.6 %all-reduce = (f32[768]{0:T(1024)}, f32[3,3,768]{2,1,0:T(4,128)}, f32[5,128]{1,0:T(8,128)}, f32[128]{0:T(128)}, f32[768]{0:T(1024)}) all-reduce(f32[768]{0:T(1024)S(1)} %get-tuple-element.68, f32[3,3,768]{2,1,0:T(4,128)S(1)} %pad_maximum_fusion.3, f32[5,128]{1,0:T(8,128)S(1)} %fusion.358, ...), channel_id=1, replica_groups=mesh['seq'=16,'tp'=2] {'seq'}, use_global_device_ids=true, to_apply=%region_11.12 | all-reduce | flops 9216 | bytes 73728 | tf_op jit(solution)/shard_map/psum | solution.py:336
  419.2 95.9 %all-reduce.4.cloned.1.call-done = (f32[192,3,768]{2,0,1:T(8,128)}, f32[128,128]{1,0:T(8,128)}, f32[192,768]{1,0:T(8,128)}, f32[4,192,2,384]{3,1,2,0:T(8,128)}, f32[384,768]{1,0:T(8,128)}) async-done(((f32[192,3,768]{2,0,1:T(8,128)}, f32[128,128]{1,0:T(8,128)}, f32[192,768]{1,0:T(8,128)}, f32[4,192,2,384]{3,1,2,0:T(8,128)}, f32[384,768]{1,0:T(8,128)}), (f32[192,3,768]{2,0,1:T(8,128)}, f32[128,128]{1,0:T(8,128)}, ...) | async-done | bytes 5963792 | tf_op jit(solution)/shard_map/psum | solution.py:336
  515.1 5.0 copy.154
  (292 shorter events, 74.2 us)
Async XLA Ops:
  7.2 141.4 %copy-start = (bf16[4,192,2,384]{3,2,1,0:T(2,128)(2,1)S(1)}, bf16[4,192,2,384]{3,2,1,0:T(2,128)(2,1)}, u32[]{:S(2)}) copy-start(bf16[4,192,2,384]{3,2,1,0:T(2,128)(2,1)} %param.25) | copy-start | bytes 3538948
  8.5 3.7 copy-start.75
  8.6 3.8 copy-start.78
  9.3 3.7 copy-start.81
  13.4 8.9 %copy-start.92 = (f32[5,128]{1,0:T(8,128)S(1)}, f32[5,128]{1,0:T(8,128)}, u32[]{:S(2)}) copy-start(f32[5,128]{1,0:T(8,128)} %param.18) | copy-start | bytes 7684
  13.4 8.9 %copy-start.93 = (f32[128]{0:T(128)S(1)}, f32[128]{0:T(128)}, u32[]{:S(2)}) copy-start(f32[128]{0:T(128)} %param.19) | copy-start | bytes 1540
  14.9 62.9 %collective-permute-start = (bf16[3,768,2]{1,2,0:T(2,128)(2,1)S(1)}, bf16[3,768,2]{1,2,0:T(2,128)(2,1)S(1)}, u32[]{:S(2)}, u32[]{:S(2)}) collective-permute-start(bf16[3,768,2]{1,2,0:T(2,128)(2,1)S(1)} %copy.123), channel_id=1, source_target_pairs={{0,2},{2,4},{4,6},{6,8},{8,10},{10,12},{12,14},{14,16},{16,18},{18... | collective-permute-start | bytes 27656 | tf_op jit(solution)/shard_map/ppermute | solution.py:19
  19.8 45.0 %copy-start.60 = (f32[8192]{0:T(1024)}, f32[8192]{0:T(1024)S(1)}, u32[]{:S(2)}) copy-start(f32[8192]{0:T(1024)S(1)} %fusion.185) | copy-start | bytes 98308
  20.0 103.2 %copy-start.21 = (f32[64,128]{1,0:T(8,128)}, f32[64,128]{1,0:T(8,128)S(1)}, u32[]{:S(2)}) copy-start(f32[64,128]{1,0:T(8,128)S(1)} %get-tuple-element.117) | copy-start | bytes 98308
  20.0 103.2 %copy-start.23 = (f32[64,128]{1,0:T(8,128)}, f32[64,128]{1,0:T(8,128)S(1)}, u32[]{:S(2)}) copy-start(f32[64,128]{1,0:T(8,128)S(1)} %get-tuple-element.118) | copy-start | bytes 98308
  22.3 22.7 %copy-start.51 = (f32[8192,5]{0,1:T(8,128)}, f32[8192,5]{0,1:T(8,128)S(1)}, u32[]{:S(2)}) copy-start(f32[8192,5]{0,1:T(8,128)S(1)} %stack.38) | copy-start | bytes 491524
  22.3 22.7 %copy-start.66 = (f32[128,128]{1,0:T(8,128)S(1)}, f32[128,128]{1,0:T(8,128)}, u32[]{:S(2)}) copy-start(f32[128,128]{1,0:T(8,128)} %param.20) | copy-start | bytes 196612
  44.9 19.8 %copy-start.6 = (f32[8192,128]{1,0:T(8,128)}, f32[8192,128]{1,0:T(8,128)S(1)}, u32[]{:S(2)}) copy-start(f32[8192,128]{1,0:T(8,128)S(1)} %get-tuple-element.106) | copy-start | bytes 12582916
  45.0 19.8 %copy-start.72 = (f32[128,48]{0,1:T(8,128)S(1)}, f32[128,48]{0,1:T(8,128)}, u32[]{:S(2)}) copy-start(f32[128,48]{0,1:T(8,128)} %param.21) | copy-start | bytes 73732
  45.0 19.8 %copy-start.88 = (f32[48]{0:T(128)S(1)}, f32[48]{0:T(128)}, u32[]{:S(2)}) copy-start(f32[48]{0:T(128)} %param.22) | copy-start | bytes 580
  64.8 4.6 copy-start.4
  73.0 8.1 %copy-start.68 = (f32[3,768]{1,0:T(4,128)}, f32[3,768]{1,0:T(4,128)S(1)}, u32[]{:S(2)}) copy-start(f32[3,768]{1,0:T(4,128)S(1)} %get-tuple-element.104) | copy-start | bytes 27652
  73.0 8.1 %copy-start.70 = (f32[3,768]{1,0:T(4,128)}, f32[3,768]{1,0:T(4,128)S(1)}, u32[]{:S(2)}) copy-start(f32[3,768]{1,0:T(4,128)S(1)} %get-tuple-element.105) | copy-start | bytes 27652
  77.8 45.4 %copy-start.62 = (f32[64,64]{0,1:T(8,128)}, f32[64,64]{0,1:T(8,128)S(1)}, u32[]{:S(2)}) copy-start(f32[64,64]{0,1:T(8,128)S(1)} %fusion.227) | copy-start | bytes 49156
  81.1 2.4 copy-start.2
  85.4 18.4 %all-to-all-start = ((bf16[16,48,256]{2,1,0:T(8,128)(2,1)}), bf16[16,48,256]{2,1,0:T(8,128)(2,1)}, u32[]{:S(2)}, u32[]{:S(2)}) async-start(bf16[16,48,256]{2,1,0:T(8,128)(2,1)} %bitcast.465), calls=%async_computation | async-start | bytes 786432 | tf_op jit(solution)/shard_map/all_to_all | solution.py:189
  91.9 30.0 %copy-start.64 = (f32[64,64]{0,1:T(8,128)}, f32[64,64]{0,1:T(8,128)S(1)}, u32[]{:S(2)}) copy-start(f32[64,64]{0,1:T(8,128)S(1)} %fusion.226) | copy-start | bytes 49156
  91.9 3.2 copy-start.8
  111.9 3.3 copy-start.14
  127.2 7.5 %copy-start.58 = (bf16[128,768]{1,0:T(8,128)(2,1)S(1)}, bf16[128,768]{1,0:T(8,128)(2,1)}, u32[]{:S(2)}) copy-start(bf16[128,768]{1,0:T(8,128)(2,1)} %param.27) | copy-start | bytes 589828
  127.2 15.8 %all-to-all-start.1 = ((bf16[48,16,256]{2,0,1:T(8,128)(2,1)}), bf16[48,16,256]{2,0,1:T(8,128)(2,1)}, u32[]{:S(2)}, u32[]{:S(2)}) async-start(bf16[48,16,256]{2,0,1:T(8,128)(2,1)} %copy.130), calls=%async_computation.1 | async-start | bytes 786432 | tf_op jit(solution)/shard_map/all_to_all | solution.py:209
  131.5 34.8 %reduce-scatter.5.cloned.1.call-start = ((), (), s32[]{:S(2)}) async-start(), calls=%async_computation.7 | async-start | bytes 1179648 | tf_op jit(solution)/shard_map/reduce_scatter | solution.py:248
  138.0 5.0 copy-start.40
  145.7 2.9 copy-start.84
  156.7 21.4 %reduce-scatter.3.cloned.1.call-start = ((), (), s32[]{:S(2)}) async-start(), calls=%async_computation.6 | async-start | bytes 1179648 | tf_op jit(solution)/shard_map/reduce_scatter | solution.py:226
  156.8 4.5 copy-start.32
  156.8 4.5 copy-start.41
  162.7 3.6 copy-start.85
  162.7 4.9 copy-start.95
  162.7 4.9 copy-start.91
  162.7 15.4 %copy-start.57 = (bf16[128,768]{0,1:T(8,128)(2,1)S(1)}, bf16[128,768]{0,1:T(8,128)(2,1)}, u32[]{:S(2)}) copy-start(bf16[128,768]{0,1:T(8,128)(2,1)} %copy.135) | copy-start | bytes 589828
  166.3 11.8 %copy-start.42 = (f32[128,768]{0,1:T(8,128)S(1)}, f32[128,768]{0,1:T(8,128)}, u32[]{:S(2)}) copy-start(f32[128,768]{0,1:T(8,128)} %reduce-scatter.5.cloned.1.call-done) | copy-start | bytes 1179652
  180.0 3.5 copy-start.44
  183.7 8.9 %copy-start.39 = (bf16[256,768]{0,1:T(8,128)(2,1)S(1)}, bf16[256,768]{0,1:T(8,128)(2,1)}, u32[]{:S(2)}) copy-start(bf16[256,768]{0,1:T(8,128)(2,1)} %copy-done.38) | copy-start | bytes 1179652
  185.4 19.9 %all-to-all-start.2 = ((bf16[16,48,256]{2,1,0:T(8,128)(2,1)}), bf16[16,48,256]{2,1,0:T(8,128)(2,1)}, u32[]{:S(2)}, u32[]{:S(2)}) async-start(bf16[16,48,256]{2,1,0:T(8,128)(2,1)} %multiply_convert_fusion.1), calls=%async_computation.4 | async-start | bytes 786432 | tf_op jit(solution)/shard_map/all_to_all | solution.py:273
  192.6 3.4 copy-start.46
  196.0 3.4 copy-start.31
  199.4 7.3 %copy-start.65 = (f32[64,64]{0,1:T(8,128)S(1)}, f32[64,64]{0,1:T(8,128)}, u32[]{:S(2)}) copy-start(f32[64,64]{0,1:T(8,128)} %copy-done.64) | copy-start | bytes 49156
  211.8 2.3 copy-start.33
  235.1 32.1 %all-to-all-start.3 = ((bf16[48,16,256]{2,0,1:T(8,128)(2,1)}), bf16[48,16,256]{2,0,1:T(8,128)(2,1)S(1)}, u32[]{:S(2)}, u32[]{:S(2)}) async-start(bf16[48,16,256]{2,0,1:T(8,128)(2,1)} %copy.141), calls=%async_computation.5 | async-start | bytes 786432 | tf_op jit(solution)/shard_map/all_to_all | solution.py:301
  238.8 276.3 %all-reduce.4.cloned.1.call-start = ((), (), s32[]{:S(2)}) async-start(), calls=%async_computation.8 | async-start | bytes 11927552 | tf_op jit(solution)/shard_map/psum | solution.py:336
  238.8 3.4 copy-start.17
  242.2 3.3 copy-start.9
  242.2 3.2 copy-start.61
  242.2 3.2 copy-start.73
  242.3 3.2 copy-start.89
  271.7 12.5 %collective-permute-start.1 = (f32[3,768,2]{1,2,0:T(2,128)S(1)}, f32[3,768,2]{1,2,0:T(2,128)S(1)}, u32[]{:S(2)}, u32[]{:S(2)}) collective-permute-start(f32[3,768,2]{1,2,0:T(2,128)S(1)} %copy.142), channel_id=1, source_target_pairs={{2,0},{4,2},{6,4},{8,6},{10,8},{12,10},{14,12},{16,14},{18,16},{20... | collective-permute-start | bytes 55304 | tf_op jit(solution)/shard_map/ppermute | solution.py:19
  285.7 2.4 copy-start.3
  285.7 2.4 copy-start.69
  285.7 2.4 copy-start.71
  288.0 6.0 %copy-start.48 = (bf16[256,768]{0,1:T(8,128)(2,1)S(1)}, bf16[256,768]{0,1:T(8,128)(2,1)}, u32[]{:S(2)}) copy-start(bf16[256,768]{0,1:T(8,128)(2,1)} %copy-done.47) | copy-start | bytes 1179652
  303.9 3.7 copy-start.67
  307.7 20.5 %copy-start.52 = (f32[8192,5]{0,1:T(8,128)S(1)}, f32[8192,5]{0,1:T(8,128)}, u32[]{:S(2)}) copy-start(f32[8192,5]{0,1:T(8,128)} %copy-done.51) | copy-start | bytes 491524
  307.7 22.6 %copy-start.19 = (f32[48,128,64]{1,2,0:T(8,128)S(1)}, f32[48,128,64]{1,2,0:T(8,128)}, u32[]{:S(2)}) copy-start(f32[48,128,64]{1,2,0:T(8,128)} %copy-done.18) | copy-start | bytes 4718596
  330.5 4.1 copy-start.35
  330.5 4.1 copy-start.37
  515.1 5.0 copy-start.53
  520.1 2.7 copy-start.55
  521.3 2.5 copy-start.1
  (41 other events, 53.8 us)
Sparse Core Ops, SparseCore 0:
  156.9 9.4 reduce-scatter.4
  168.7 9.3 reduce-scatter.2
  304.1 210.9 all-reduce.3
where the time goes:
time: 538 us; the launch traced here: 531 us
  matrix products  189 us (35%)
  waiting for transfers between devices  115 us (21%)
  blocking collectives  90.3 us (17%)
  local copies, waits for them, and re-layouts  58.8 us (11%)
  other arithmetic  33.5 us (6%)
  starting transfers between devices  28.2 us (5%)
  between operations  15.4 us (3%)
    psum x1, waiting for transfers between devices, local(): lax.psum((mixer_gain_grad, in_proj_grad, short_taps_grad, weight_first_gr...  95.9 us
    psum x1, blocking collectives, local(): lax.psum((mixer_gain_grad, in_proj_grad, short_taps_grad, weight_first_gr...  81.6 us
    dot_general x3, matrix products, filter_taps(): jnp.dot(hidden_first, weight_second, precision=EXACT_PRODUCT)  51.1 us
    dot_general x3, matrix products, filter_taps(): shaped = jnp.dot(hidden_second, weight_third, precision=EXACT_PRODUCT)  30.4 us
    unnamed x204, local copies, waits for them, and re-layouts  28.1 us
    dot_general x2, matrix products, filter_taps(): jnp.dot(features, weight_first, precision=EXACT_PRODUCT) + bias_first  24.8 us
  transfers between devices with their start and end apart: 9, of which 5 were waited for; matrix products, arithmetic and copies ran while one was open for 30% of the time, Pallas kernels for 0%

commit v1 on v0

v1 whole, which is shorter than its diff:
```python
import math
import functools

import jax
import jax.numpy as jnp
import ml_dtypes
import numpy as np
from jax import lax
from jax.experimental import pallas as pl
from jax.experimental.pallas import tpu as pltpu
from jax.sharding import PartitionSpec as P

MIN_LEN = 8192
EPSILON = 1e-05
LANES = 128
GROUP = 8
VMEM_BYTES = 60 * 1024 * 1024
BF = jnp.bfloat16
F32 = jnp.float32

PI_HIGH = 3.140625
PI_LOW = 9.67653589793e-4
SIN_C = (1.0, -0.16666647791862488, 0.00833289884030819, -0.0001980081869987771, 2.590327312645968e-06)
COS_C = (0.9999999403953552, -0.4999990463256836, 0.041663575917482376, -0.0013853635173290968, 2.315232813998591e-05)


def vmem_specs(count):
    return [pl.BlockSpec(memory_space=pltpu.VMEM)] * count


def params(flops=0):
    return pltpu.CompilerParams(vmem_limit_bytes=VMEM_BYTES)


def cost(flops, bytes_accessed=0, transcendentals=0):
    return pl.CostEstimate(flops=flops, bytes_accessed=bytes_accessed, transcendentals=transcendentals)


def split_np(table):
    high = np.asarray(table, np.float32).astype(ml_dtypes.bfloat16)
    low = (np.asarray(table, np.float64) - high.astype(np.float64)).astype(ml_dtypes.bfloat16)
    return high, low


def split3_np(table):
    table = np.asarray(table, np.float64)
    high = table.astype(np.float32).astype(ml_dtypes.bfloat16)
    rest = table - high.astype(np.float64)
    mid = rest.astype(np.float32).astype(ml_dtypes.bfloat16)
    low = (rest - mid.astype(np.float64)).astype(np.float32).astype(ml_dtypes.bfloat16)
    return high, mid, low


@functools.lru_cache(maxsize=None)
def transform_tables(seq_length):
    period = 2 * seq_length
    first = period // LANES
    kept = first // 2 + 1
    padded = -(-kept // 8) * 8
    k = np.arange(padded)
    live = (k < kept).astype(np.float64)
    n = np.arange(first)
    angle = 2 * np.pi / first * ((k[:, None] * n[None, :]) % first)
    eye = np.eye(GROUP)
    stage = np.zeros((GROUP, 2, padded, first, GROUP))
    stage[:, 0] = np.einsum("kn,cd->cknd", np.cos(angle) * live[:, None], eye)
    stage[:, 1] = np.einsum("kn,cd->cknd", -np.sin(angle) * live[:, None], eye)
    forward = stage.reshape(GROUP * 2 * padded, first * GROUP)
    backward = forward.T
    m = np.arange(LANES)
    turn = 2 * np.pi / period * ((k[:, None] * m[None, :]) % period)
    weight = np.where((k == 0) | (k == first // 2), 1.0, 2.0) * live / period
    twiddle = np.stack(
        [np.cos(turn), np.sin(turn), np.cos(turn) * weight[:, None], np.sin(turn) * weight[:, None]]
    ).astype(np.float32)
    inner = 2 * np.pi / LANES * ((m[:, None] * m[None, :]) % LANES)
    c, s = np.cos(inner), np.sin(inner)
    second = np.block([[c, -s], [s, c]])
    return {
        "forward": split_np(forward),
        "backward": split_np(backward),
        "twiddle": twiddle,
        "second": split_np(second),
        "inverse": split_np(second.T),
        "first": first,
        "padded": padded,
    }


@functools.lru_cache(maxsize=None)
def feature_table(seq_length):
    period = 2 * seq_length
    index = np.arange(period)
    lag = np.where(index < seq_length, index, index - period)
    q = lag / seq_length
    rows = [q, np.cos(2 * np.pi * q), np.cos(4 * np.pi * q), np.sin(2 * np.pi * q), np.sin(4 * np.pi * q)]
    rows.append(np.ones_like(q))
    rows += [np.zeros_like(q)] * 2
    high, mid, low = split3_np(np.stack(rows))
    return np.concatenate([high, high, mid, high, mid, low], axis=0)


def split(values):
    high = values.astype(BF)
    low = (values - high.astype(F32)).astype(BF)
    return high, low


def first_weights(rows):
    high = rows.astype(BF).astype(F32)
    mid = (rows - high).astype(BF).astype(F32)
    low = rows - high - mid
    return jnp.concatenate([high, mid, high, low, mid, high], axis=0).astype(BF)


def mm(a, b):
    return jnp.dot(a, b, preferred_element_type=F32)


def mm_nt(a, b):
    return lax.dot_general(a, b, (((1,), (1,)), ((), ())), preferred_element_type=F32)


def mm_tn(a, b):
    return lax.dot_general(a, b, (((0,), (0,)), ((), ())), preferred_element_type=F32)


def mm3(a, b):
    ah, al = a
    bh, bl = b
    return mm(ah, bh) + (mm(al, bh) + mm(ah, bl))


def mm3_tn(a, b):
    ah, al = a
    bh, bl = b
    return mm_tn(ah, bh) + (mm_tn(al, bh) + mm_tn(ah, bl))


def sine_cosine(x):
    n = jnp.round(x * (1.0 / math.pi))
    r = (x - n * PI_HIGH) - n * PI_LOW
    half = n * 0.5
    sign = 1.0 - 4.0 * (half - jnp.floor(half))
    r2 = r * r
    s = SIN_C[4]
    for c in SIN_C[3::-1]:
        s = s * r2 + c
    k = COS_C[4]
    for c in COS_C[3::-1]:
        k = k * r2 + c
    return s * (r * sign), k * sign


def lag_decay(decay, start, width, seq_length):
    lane = lax.broadcasted_iota(jnp.int32, decay.shape[:1] + (width,), 1) + start
    lag = jnp.where(lane < seq_length, lane, 2 * seq_length - lane).astype(F32)
    return jnp.exp(lag * (decay[:, :1] * (-1.0 / seq_length)))


def filter_forward_kernel(seq_length, feat_ref, w1_ref, w2_ref, w3_ref, decay_ref, lag_ref, a_ref, ac_ref, b_ref, bc_ref):
    width = feat_ref.shape[1]
    start = pl.program_id(0) * width
    pre = mm_tn(first_weights(w1_ref[...]), feat_ref[...])
    s1, c1 = sine_cosine(pre)
    a_ref[...] = s1.astype(BF)
    ac_ref[...] = c1.astype(BF)
    pre2 = mm3_tn(split(w2_ref[...]), split(s1))
    s2, c2 = sine_cosine(pre2)
    b_ref[...] = s2.astype(BF)
    bc_ref[...] = c2.astype(BF)
    shaped = mm3(split(w3_ref[...]), split(s2))
    lag_ref[...] = shaped * lag_decay(decay_ref[...], start, width, seq_length)


def filter_forward(features, w1b, w2, w3t, decay, seq_length):
    hidden = w2.shape[0]
    channels = w3t.shape[0]
    period = features.shape[1]
    width = 1024
    whole = lambda a: pl.BlockSpec(a.shape, lambda i: (0, 0))
    lanes = lambda rows: pl.BlockSpec((rows, width), lambda i: (0, i))
    return pl.pallas_call(
        functools.partial(filter_forward_kernel, seq_length),
        grid=(period // width,),
        in_specs=[lanes(features.shape[0]), whole(w1b), whole(w2), whole(w3t), whole(decay)],
        out_specs=[lanes(channels)] + [lanes(hidden)] * 4,
        out_shape=[jax.ShapeDtypeStruct((channels, period), F32)]
        + [jax.ShapeDtypeStruct((hidden, period), BF)] * 4,
        compiler_params=params(),
        cost_estimate=cost(2 * period * hidden * (hidden * 3 + 48 + 72), 4 * period * hidden * 2, 0),
        name="filter_forward",
    )(features, w1b, w2, w3t, decay)


def filter_backward_kernel(seq_length, grad_ref, feat_ref, w2_ref, w3_ref, decay_ref, a_ref, ac_ref, b_ref, bc_ref, g1_ref, g2_ref, g3_ref):
    width = grad_ref.shape[1]
    step = pl.program_id(0)

    @pl.when(step == 0)
    def _():
        g1_ref[...] = jnp.zeros_like(g1_ref)
        g2_ref[...] = jnp.zeros_like(g2_ref)
        g3_ref[...] = jnp.zeros_like(g3_ref)

    weighted = grad_ref[...] * lag_decay(decay_ref[...], step * width, width, seq_length)
    wh, wl = split(weighted)
    second = b_ref[...]
    g3_ref[...] += mm_nt(wh, second) + mm_nt(wl, second)
    pre2 = mm3_tn(split(w3_ref[...]), (wh, wl)) * bc_ref[...].astype(F32)
    ph, plow = split(pre2)
    first = a_ref[...]
    g2_ref[...] += mm_nt(first, ph) + mm_nt(first, plow)
    pre1 = mm3(split(w2_ref[...]), (ph, plow)) * ac_ref[...].astype(F32)
    qh, ql = split(pre1)
    feat = feat_ref[...]
    g1_ref[...] += mm_nt(feat, qh) + mm_nt(feat, ql)


def filter_backward(grad, features, w2, w3t, decay, saved, seq_length):
    hidden = w2.shape[0]
    channels, period = grad.shape
    width = 1024
    whole = lambda a: pl.BlockSpec(a.shape, lambda i: (0, 0))
    lanes = lambda rows: pl.BlockSpec((rows, width), lambda i: (0, i))
    out = lambda r, c: pl.BlockSpec((r, c), lambda i: (0, 0))
    return pl.pallas_call(
        functools.partial(filter_backward_kernel, seq_length),
        grid=(period // width,),
        in_specs=[lanes(channels), lanes(8), whole(w2), whole(w3t), whole(decay)] + [lanes(hidden)] * 4,
        out_specs=[out(8, hidden), out(hidden, hidden), out(channels, hidden)],
        out_shape=[
            jax.ShapeDtypeStruct((8, hidden), F32),
            jax.ShapeDtypeStruct((hidden, hidden), F32),
            jax.ShapeDtypeStruct((channels, hidden), F32),
        ],
        compiler_params=params(),
        cost_estimate=cost(2 * period * hidden * (hidden * 5 + 200), 4 * period * hidden * 2, 0),
        name="filter_backward",
    )(grad, features, w2, w3t, decay, *saved)


def spectrum_of(x_pair, fwd, twiddle_ref, second, padded, columns):
    if x_pair[1] is None:
        a = mm(fwd[0], x_pair[0]) + mm(fwd[1], x_pair[0])
    else:
        a = mm3(fwd, x_pair)
    tc, ts = twiddle_ref[0], twiddle_ref[1]
    parts = []
    for col in range(columns):
        lanes = slice(col * LANES, (col + 1) * LANES)
        for c in range(GROUP):
            base = c * 2 * padded
            re = a[base : base + padded, lanes]
            im = a[base + padded : base + 2 * padded, lanes]
            parts.append(jnp.concatenate([re * tc + im * ts, im * tc - re * ts], axis=1))
    return mm3(split(jnp.concatenate(parts, axis=0)), second)


def signal_of(spec, inverse, twiddle_ref, back, padded, columns):
    b = mm3(split(spec), inverse)
    tc, ts = twiddle_ref[2], twiddle_ref[3]
    cols = []
    for col in range(columns):
        parts = []
        for c in range(GROUP):
            base = (col * GROUP + c) * padded
            re = b[base : base + padded, :LANES]
            im = b[base : base + padded, LANES:]
            parts.append(re * tc - im * ts)
            parts.append(im * tc + re * ts)
        cols.append(jnp.concatenate(parts, axis=0))
    z = jnp.concatenate(cols, axis=1)
    return mm3(back, split(z))


def gathered(x_ref, seqs, rows, groups):
    cols = []
    for q in range(seqs):
        for g in range(groups):
            block = x_ref[q * rows : (q + 1) * rows, g * GROUP : (g + 1) * GROUP, :].astype(F32)
            cols.append(block.reshape(rows * GROUP, LANES))
    return jnp.concatenate(cols, axis=1)


def scattered(y_ref, y, seqs, rows, groups):
    for q in range(seqs):
        for g in range(groups):
            col = q * groups + g
            block = y[:, col * LANES : (col + 1) * LANES].reshape(rows, GROUP, LANES)
            y_ref[q * rows : (q + 1) * rows, g * GROUP : (g + 1) * GROUP, :] = block.astype(y_ref.dtype)


def product(a, b, conjugate):
    ar, ai = a[:, :LANES], a[:, LANES:]
    br, bi = b[:, :LANES], b[:, LANES:]
    if conjugate:
        return jnp.concatenate([ar * br + ai * bi, ai * br - ar * bi], axis=1)
    return jnp.concatenate([ar * br - ai * bi, ar * bi + ai * br], axis=1)


def filter_spectrum_kernel(padded, lag_ref, fh, fl, tw, sh, sl, out_ref):
    groups = lag_ref.shape[0] // GROUP
    first = lag_ref.shape[1] // LANES
    cols = []
    for g in range(groups):
        rows = [lag_ref[g * GROUP : (g + 1) * GROUP, n * LANES : (n + 1) * LANES] for n in range(first)]
        cols.append(jnp.concatenate(rows, axis=0))
    x = jnp.concatenate(cols, axis=1)
    out_ref[...] = spectrum_of(split(x), (fh[...], fl[...]), tw, (sh[...], sl[...]), padded, groups)


def conv_forward_kernel(padded, seqs, x_ref, h_ref, fh, fl, tw, sh, sl, ih, il, bh, bl, y_ref, spec_ref):
    rows = x_ref.shape[0] // seqs
    groups = x_ref.shape[1] // GROUP
    used = rows * GROUP
    x = gathered(x_ref, seqs, rows, groups).astype(BF)
    spec = spectrum_of((x, None), (fh[:, :used], fl[:, :used]), tw, (sh[...], sl[...]), padded, seqs * groups)
    spec_ref[...] = spec
    h = h_ref[...]
    prod = product(spec, jnp.concatenate([h] * seqs, axis=0), False)
    y = signal_of(prod, (ih[...], il[...]), tw, (bh[:used, :], bl[:used, :]), padded, seqs * groups)
    scattered(y_ref, y, seqs, rows, groups)


def conv_backward_kernel(padded, seqs, x_ref, h_ref, fh, fl, tw, sh, sl, ih, il, bh, bl, y_ref, spec_ref):
    rows = x_ref.shape[0] // seqs
    groups = x_ref.shape[1] // GROUP
    used = rows * GROUP
    x = gathered(x_ref, seqs, rows, groups).astype(BF)
    spec = spectrum_of((x, None), (fh[:, :used], fl[:, :used]), tw, (sh[...], sl[...]), padded, seqs * groups)
    spec_ref[...] = spec
    h = h_ref[...]
    prod = product(spec, jnp.concatenate([h] * seqs, axis=0), True)
    y = signal_of(prod, (ih[...], il[...]), tw, (bh[:used, :], bl[:used, :]), padded, seqs * groups)
    scattered(y_ref, y, seqs, rows, groups)


def filter_grad_kernel(padded, seqs, spec_ref, saved_ref, tw, ih, il, bh, bl, out_ref):
    groups = out_ref.shape[0] // GROUP
    first = out_ref.shape[1] // LANES
    height = groups * GROUP * padded
    total = None
    for q in range(seqs):
        rows = slice(q * height, (q + 1) * height)
        part = product(spec_ref[rows, :], saved_ref[rows, :], True)
        total = part if total is None else total + part
    y = signal_of(total, (ih[...], il[...]), tw, (bh[...], bl[...]), padded, groups)
    for g in range(groups):
        for n in range(first):
            out_ref[g * GROUP : (g + 1) * GROUP, n * LANES : (n + 1) * LANES] = y[
                n * GROUP : (n + 1) * GROUP, g * LANES : (g + 1) * LANES
            ]


def filter_spectrum(lag, tables):
    padded = tables["padded"]
    return pl.pallas_call(
        functools.partial(filter_spectrum_kernel, padded),
        in_specs=vmem_specs(6),
        out_specs=vmem_specs(1)[0],
        out_shape=jax.ShapeDtypeStruct((lag.shape[0] * padded, 2 * LANES), F32),
        compiler_params=params(),
        cost_estimate=cost(2 * 10**9, 4 * 10**6),
        name="filter_spectrum",
    )(lag, *tables["forward"], tables["twiddle"], *tables["second"])


def conv_call(kernel, name, x, spectrum, tables, seqs):
    padded = tables["padded"]
    rows = seqs * x.shape[1] * padded
    return pl.pallas_call(
        functools.partial(kernel, padded, seqs),
        in_specs=vmem_specs(11),
        out_specs=vmem_specs(2),
        out_shape=[
            jax.ShapeDtypeStruct(x.shape, BF),
            jax.ShapeDtypeStruct((rows, 2 * LANES), F32),
        ],
        compiler_params=params(),
        cost_estimate=cost(4 * 10**9, 6 * 10**6),
        name=name,
    )(x, spectrum, *tables["forward"], tables["twiddle"], *tables["second"], *tables["inverse"], *tables["backward"])


def filter_grad_of(spec, saved, channels, seq_length, tables, seqs):
    padded = tables["padded"]
    return pl.pallas_call(
        functools.partial(filter_grad_kernel, padded, seqs),
        in_specs=vmem_specs(7),
        out_specs=vmem_specs(1)[0],
        out_shape=jax.ShapeDtypeStruct((channels, 2 * seq_length), F32),
        compiler_params=params(),
        cost_estimate=cost(3 * 10**9, 6 * 10**6),
        name="filter_grad",
    )(spec, saved, tables["twiddle"], *tables["inverse"], *tables["backward"])


def erf_parts(g):
    x = jnp.abs(g) * (1.0 / math.sqrt(2.0))
    t = 1.0 / (1.0 + 0.3275911 * x)
    e = jnp.exp(-x * x)
    poly = t * (0.254829592 + t * (-0.284496736 + t * (1.421413741 + t * (-1.453152027 + t * 1.061405429))))
    tail = 0.5 * poly * e
    return jnp.where(g < 0, tail, 1.0 - tail), e


def norm_stats(v):
    centered = v - jnp.mean(v, axis=-1, keepdims=True)
    variance = jnp.mean(centered * centered, axis=-1, keepdims=True)
    r = lax.rsqrt(variance + EPSILON)
    return centered * r, r


def norm_backward(w, gain, xhat, r):
    a = w * gain
    return r * (a - jnp.mean(a, axis=-1, keepdims=True) - xhat * jnp.mean(a * xhat, axis=-1, keepdims=True))


def column(j, width):
    return slice(j * width, (j + 1) * width)


def mixer_in_kernel(x_ref, halo_ref, gain_ref, w_ref, taps_ref, conv_ref, n1_ref, proj_ref, sm2_ref):
    rows = x_ref.shape[0]
    width = w_ref.shape[1]
    blocks = w_ref.shape[2] // width
    lead = halo_ref.shape[0]
    x = jnp.concatenate([halo_ref[...].astype(F32), x_ref[...].astype(F32)], axis=0)
    xhat, _ = norm_stats(x)
    n1 = (xhat * gain_ref[...]).astype(BF)
    n1_ref[...] = n1[lead:]
    mixed = []
    for p in range(3):
        proj = jnp.concatenate(
            [mm(n1[:, column(j, width)], w_ref[p, :, column(j, width)]) for j in range(blocks)], axis=1
        ).astype(BF)
        proj_ref[p] = proj
        proj = proj.astype(F32)
        mixed.append(
            taps_ref[0, p : p + 1, :] * proj[lead:]
            + taps_ref[1, p : p + 1, :] * proj[lead - 1 : lead - 1 + rows]
            + taps_ref[2, p : p + 1, :] * proj[lead - 2 : lead - 2 + rows]
        )
    sm2_ref[...] = mixed[2]
    conv_ref[...] = (mixed[0] * mixed[1]).T.astype(BF)


def mixer_in(x, halo, gain, w, taps):
    rows, width = x.shape
    lead = halo.shape[0]
    return pl.pallas_call(
        mixer_in_kernel,
        in_specs=vmem_specs(5),
        out_specs=vmem_specs(4),
        out_shape=[
            jax.ShapeDtypeStruct((width, rows), BF),
            jax.ShapeDtypeStruct((rows, width), BF),
            jax.ShapeDtypeStruct((3, lead + rows, width), BF),
            jax.ShapeDtypeStruct((rows, width), F32),
        ],
        compiler_params=params(),
        cost_estimate=cost(3 * 10**9, 4 * 10**6),
        name="mixer_in",
    )(x, halo, gain, w, taps)


def glu_block(x, og, w_pairs, d_pairs):
    down = None
    back = None
    kept = []
    for (wg, wu), wd in zip(w_pairs, d_pairs):
        gate = mm(x, wg)
        up = mm(x, wu)
        phi, e = erf_parts(gate)
        act = gate * phi
        hidden = (act * up).astype(BF)
        hg = mm_nt(og, wd)
        slope = phi + gate * (e * (1.0 / math.sqrt(2.0 * math.pi)))
        gg = (hg * up * slope).astype(BF)
        ug = (hg * act).astype(BF)
        kept.append((hidden, gg, ug))
        if x is not None:
            down_part = mm(hidden, wd)
            back_part = mm_nt(gg, wg) + mm_nt(ug, wu)
            down = down_part if down is None else down + down_part
            back = back_part if back is None else back + back_part
    return down, back, kept


def middle_kernel(conv_ref, sm2_ref, x_ref, og_ref, gain_ref, wo_ref, ga_ref, gb_ref, da_ref, db_ref,
                  cg_ref, third_ref, mid_ref, out_ref, n2_ref, wog_ref, gg_ref):
    width = wo_ref.shape[0]
    blocks = wo_ref.shape[1] // width
    conv = conv_ref[...].astype(F32).T
    sm2 = sm2_ref[...]
    gated = (sm2 * conv).astype(BF)
    branch = jnp.concatenate(
        [mm(gated[:, column(j, width)], wo_ref[:, column(j, width)]) for j in range(blocks)], axis=1
    )
    middle = x_ref[...].astype(F32) + branch
    xhat, r = norm_stats(middle)
    n2 = (xhat * gain_ref[...]).astype(BF)
    n2_ref[...] = n2.astype(F32).T.astype(BF)
    og = og_ref[...]
    downs, backs = [], []
    for j in range(blocks):
        down, back, _ = glu_block(
            n2[:, column(j, width)],
            og[:, column(j, width)],
            [(ga_ref[j, 0], ga_ref[j, 1]), (gb_ref[j, 0], gb_ref[j, 1])],
            [da_ref[j], db_ref[j]],
        )
        downs.append(down)
        backs.append(back)
    out_ref[...] = (middle + jnp.concatenate(downs, axis=1)).astype(BF)
    n2_grad = jnp.concatenate(backs, axis=1)
    gg_ref[...] = jnp.sum(n2_grad * xhat, axis=0, keepdims=True)
    mid_grad = og.astype(F32) + norm_backward(n2_grad, gain_ref[...], xhat, r)
    mid_ref[...] = mid_grad
    bg = mid_grad.astype(BF)
    gated_grad = jnp.concatenate(
        [mm_nt(bg[:, column(j, width)], wo_ref[:, column(j, width)]) for j in range(blocks)], axis=1
    )
    third_ref[...] = gated_grad * conv
    cg_ref[...] = (gated_grad * sm2).T.astype(BF)
    wog_ref[...] = jnp.concatenate(
        [mm_tn(gated[:, column(j, width)], bg[:, column(j, width)]) for j in range(blocks)], axis=1
    )


def middle_part(conv, sm2, x, og, gain, wo, ga, gb, da, db):
    rows, width = x.shape
    return pl.pallas_call(
        middle_kernel,
        in_specs=vmem_specs(10),
        out_specs=vmem_specs(7),
        out_shape=[
            jax.ShapeDtypeStruct((width, rows), BF),
            jax.ShapeDtypeStruct((rows, width), F32),
            jax.ShapeDtypeStruct((rows, width), F32),
            jax.ShapeDtypeStruct((rows, width), BF),
            jax.ShapeDtypeStruct((width, rows), BF),
            jax.ShapeDtypeStruct(wo.shape, F32),
            jax.ShapeDtypeStruct((1, width), F32),
        ],
        compiler_params=params(),
        cost_estimate=cost(9 * 10**9, 6 * 10**6),
        name="middle_part",
    )(conv, sm2, x, og, gain, wo, ga, gb, da, db)


def glu_grad_kernel(per_plane, x_ref, og_ref, ga_ref, gb_ref, da_ref, db_ref, own_ref, other_ref):
    j = lax.div(lax.axis_index("seq"), per_plane)
    parts = x_ref.shape[0]
    xt = jnp.concatenate([x_ref[k].astype(F32) for k in range(parts)], axis=1)
    ot = jnp.concatenate([og_ref[k].astype(F32) for k in range(parts)], axis=1)
    x = xt.T.astype(BF)
    og = ot.T.astype(BF)
    xt = xt.astype(BF)
    ot = ot.astype(BF)
    width = xt.shape[0]
    for g_ref, d_ref, out_ref in ((ga_ref, da_ref, own_ref), (gb_ref, db_ref, other_ref)):
        wg, wu, wd = g_ref[j, 0], g_ref[j, 1], d_ref[j]
        gate = mm(x, wg)
        up = mm(x, wu)
        phi, e = erf_parts(gate)
        act = gate * phi
        hidden = (act * up).astype(BF)
        hg = mm_nt(og, wd)
        slope = phi + gate * (e * (1.0 / math.sqrt(2.0 * math.pi)))
        out_ref[0:width, :] = mm(xt, (hg * up * slope).astype(BF)).astype(out_ref.dtype)
        out_ref[width : 2 * width, :] = mm(xt, (hg * act).astype(BF)).astype(out_ref.dtype)
        out_ref[2 * width :, :] = mm(ot, hidden).astype(out_ref.dtype)


def glu_grads(x, og, ga, gb, da, db, per_plane):
    width = x.shape[1]
    half = ga.shape[3]
    return pl.pallas_call(
        functools.partial(glu_grad_kernel, per_plane),
        in_specs=vmem_specs(6),
        out_specs=vmem_specs(2),
        out_shape=[
            jax.ShapeDtypeStruct((3 * width, half), F32),
            jax.ShapeDtypeStruct((3 * width, half), BF),
        ],
        compiler_params=params(),
        cost_estimate=cost(9 * 10**9, 4 * 10**6),
        name="glu_grads",
    )(x, og, ga, gb, da, db)


def short_mix(proj_ref, taps_ref, p, rows):
    lead = proj_ref.shape[1] - rows
    proj = proj_ref[p].astype(F32)
    return (
        taps_ref[0, p : p + 1, :] * proj[lead:]
        + taps_ref[1, p : p + 1, :] * proj[lead - 1 : lead - 1 + rows]
        + taps_ref[2, p : p + 1, :] * proj[lead - 2 : lead - 2 + rows]
    )


def short_grad_kernel(icg_ref, third_ref, proj_ref, taps_ref, grad_ref, halo_ref):
    rows = third_ref.shape[0]
    icg = icg_ref[...].astype(F32).T
    g0 = icg * short_mix(proj_ref, taps_ref, 1, rows)
    g1 = icg * short_mix(proj_ref, taps_ref, 0, rows)
    grad_ref[0] = g0
    grad_ref[1] = g1
    halo_ref[0] = g0[:8]
    halo_ref[1] = g1[:8]
    halo_ref[2] = third_ref[0:8, :]


def short_grads(icg, third, proj, taps):
    rows, width = third.shape
    return pl.pallas_call(
        short_grad_kernel,
        in_specs=vmem_specs(4),
        out_specs=vmem_specs(2),
        out_shape=[jax.ShapeDtypeStruct((2, rows, width), F32), jax.ShapeDtypeStruct((3, 8, width), F32)],
        compiler_params=params(),
        cost_estimate=cost(10**9, 2 * 10**6),
        name="short_grads",
    )(icg, third, proj, taps)


def mixer_back_kernel(grad_ref, third_ref, halo_ref, proj_ref, n1_ref, mid_ref, x_ref, gain_ref, w_ref, taps_ref,
                      wog_ref, gg_ref, f1_ref, f2_ref, in_ref, own_ref, other_ref, pack_ref):
    rows, model = third_ref.shape
    width = w_ref.shape[1]
    blocks = model // width
    lead = proj_ref.shape[1] - rows
    n1 = n1_ref[...]
    pack_ref[...] = jnp.zeros_like(pack_ref)
    sums = []
    back = [None] * blocks
    for p in range(3):
        g = third_ref[...] if p == 2 else grad_ref[p]
        ext = jnp.concatenate([g, halo_ref[p]], axis=0)
        proj = proj_ref[p].astype(F32)
        for k in range(3):
            sums.append(jnp.sum(g * proj[lead - k : lead - k + rows], axis=0, keepdims=True))
        pg = (
            taps_ref[0, p : p + 1, :] * g
            + taps_ref[1, p : p + 1, :] * ext[1 : rows + 1]
            + taps_ref[2, p : p + 1, :] * ext[2 : rows + 2]
        ).astype(BF)
        pack_ref[p * width : (p + 1) * width, :model] = jnp.concatenate(
            [mm_tn(n1[:, column(j, width)], pg[:, column(j, width)]) for j in range(blocks)], axis=1
        )
        for j in range(blocks):
            part = mm_nt(pg[:, column(j, width)], w_ref[p, :, column(j, width)])
            back[j] = part if back[j] is None else back[j] + part
    n1_grad = jnp.concatenate(back, axis=1)
    xhat, r = norm_stats(x_ref[...].astype(F32))
    sums.append(jnp.sum(n1_grad * xhat, axis=0, keepdims=True))
    sums.append(gg_ref[...])
    in_ref[...] = (mid_ref[...] + norm_backward(n1_grad, gain_ref[...], xhat, r)).astype(BF)
    pack_ref[3 * width : 4 * width, :model] = wog_ref[...]
    pieces = model // LANES
    hidden = f2_ref.shape[0]
    small = jnp.concatenate(sums, axis=0)
    for c in range(pieces):
        pack_ref[c * 16 : c * 16 + len(sums), model:] = small[:, c * LANES : (c + 1) * LANES]
    base = pieces * 16
    pack_ref[base : base + hidden, model:] = f2_ref[...]
    pack_ref[base + hidden : base + hidden + 8, model:] = f1_ref[...]
    half = own_ref.shape[0]
    me = lax.axis_index("tp")
    own_ref[...] = pack_ref[pl.ds(me * half, half), :]
    other_ref[...] = pack_ref[pl.ds((1 - me) * half, half), :].astype(BF)


def mixer_back(grad, third, halo, proj, n1, mid, x, gain, w, taps, wog, gg, f1, f2):
    rows, model = x.shape
    half = 2 * w.shape[1]
    return pl.pallas_call(
        mixer_back_kernel,
        in_specs=vmem_specs(14),
        out_specs=vmem_specs(3),
        out_shape=[
            jax.ShapeDtypeStruct((rows, model), BF),
            jax.ShapeDtypeStruct((half, model + LANES), F32),
            jax.ShapeDtypeStruct((half, model + LANES), BF),
        ],
        scratch_shapes=[pltpu.VMEM((2 * half, model + LANES), F32)],
        compiler_params=params(),
        cost_estimate=cost(4 * 10**9, 6 * 10**6),
        name="mixer_back",
    )(grad, third, halo, proj, n1, mid, x, gain, w, taps, wog, gg, f1, f2)


def permuted(x, axes, count, by):
    pairs = [(i, i + by) for i in range(count) if 0 <= i + by < count]
    return lax.ppermute(x, axes, pairs)


def swapped(x):
    return lax.ppermute(x, "tp", [(0, 1), (1, 0)])


def exchanged(x, axes, groups=None):
    return lax.all_to_all(x, axes, 0, 0, axis_index_groups=groups, tiled=True)


def gathered_all(x, count):
    return exchanged(jnp.broadcast_to(x[None], (count,) + x.shape), "seq")


def local(
    layer_input,
    mixer_gain,
    in_proj,
    short_taps,
    filter_w1,
    filter_b1,
    filter_w2,
    filter_w3,
    filter_decay,
    out_proj,
    glu_gain,
    glu_in,
    glu_out,
    out_grad,
):
    tok_rows, model = layer_input.shape
    width = in_proj.shape[0]
    blocks = model // width
    half = glu_out.shape[0]
    seq_devices = lax.axis_size("seq")
    tp_devices = lax.axis_size("tp")
    devices = seq_devices * tp_devices
    both = ("seq", "tp")
    rows = tok_rows // tp_devices
    seq_length = min(MIN_LEN, tok_rows * seq_devices)
    seqs = tok_rows * seq_devices // seq_length
    per_plane = seq_devices // blocks
    chans = model // devices
    chans_padded = -(-chans // GROUP) * GROUP
    tp_index = lax.axis_index("tp")
    linear = lax.axis_index("seq") * tp_devices + tp_index
    at_start = linear * rows % seq_length == 0
    at_end = (linear + 1) * rows % seq_length == 0
    tables = transform_tables(seq_length)
    features = feature_table(seq_length)
    across = [[r + g * per_plane for g in range(blocks)] for r in range(per_plane)]
    within = [[g * per_plane + r for r in range(per_plane)] for g in range(blocks)]

    own_rows = lax.dynamic_slice_in_dim(layer_input, tp_index * rows, rows, 0)
    halo = permuted(own_rows[rows - 16 :], both, devices, 1)
    halo = jnp.where(at_start, jnp.zeros_like(halo), halo)

    hidden = filter_w2.shape[0]
    w1b = jnp.concatenate([filter_w1, filter_b1[None], jnp.zeros((2, hidden), F32)], axis=0)
    pad = ((0, chans_padded - chans), (0, 0))
    w3t = jnp.pad(lax.dynamic_slice_in_dim(filter_w3.T, tp_index * chans, chans, 0), pad)
    decay = lax.dynamic_slice_in_dim(filter_decay, tp_index * chans, chans, 0)
    decay = jnp.pad(jnp.broadcast_to(decay[:, None], (chans, LANES)), pad)
    lag, *saved = filter_forward(features, w1b, filter_w2, w3t, decay, seq_length)
    spectrum = filter_spectrum(lag, tables)

    w_in = in_proj.transpose(1, 0, 2)
    conv_rows, n1, proj, sm2 = mixer_in(own_rows, halo, mixer_gain[None], w_in, short_taps)

    def to_channels(x):
        out = exchanged(x.reshape(devices, chans, rows), both)
        return jnp.pad(out, ((0, 0), (0, chans_padded - chans), (0, 0)))

    def to_tokens(x):
        return exchanged(x[:, :chans], both).reshape(model, rows)

    conv_out, signal_spec = conv_call(
        conv_forward_kernel, "conv_forward", to_channels(conv_rows), spectrum, tables, seqs
    )
    conv_tokens = to_tokens(conv_out)

    glu_own = glu_in.transpose(0, 2, 1, 3)
    down_own = glu_out.reshape(half, blocks, width).transpose(1, 0, 2)
    glu_other = swapped(glu_own)
    down_other = swapped(down_own)
    og_plane = exchanged(out_grad.T.reshape(blocks, width, rows), "seq", across)
    conv_grad, third, mid, layer_output, n2, out_grad_w, gain_two = middle_part(
        conv_tokens, sm2, own_rows, out_grad, glu_gain[None], out_proj, glu_own, glu_other, down_own, down_other
    )
    conv_grad_channels = to_channels(conv_grad)
    n2_plane = exchanged(n2.reshape(blocks, width, rows), "seq", across)

    g_own, g_other = glu_grads(n2_plane, og_plane, glu_own, glu_other, down_own, down_other, per_plane)
    glu_sum = (g_own + swapped(g_other).astype(F32)).astype(BF)
    glu_part = exchanged(glu_sum.reshape(per_plane, -1, half), "seq", within)
    glu_part = jnp.sum(glu_part.astype(F32), axis=0).astype(BF)

    input_conv_grad, grad_spec = conv_call(
        conv_backward_kernel, "conv_backward", conv_grad_channels, spectrum, tables, seqs
    )
    icg = to_tokens(input_conv_grad)
    filter_grad = filter_grad_of(grad_spec, signal_spec, chans_padded, seq_length, tables, seqs)
    g1, g2, g3 = filter_backward(filter_grad, features, filter_w2, w3t, decay, saved, seq_length)

    glu_all = gathered_all(glu_part, seq_devices).reshape(blocks, 3, width, half)

    grad01, edge = short_grads(icg, third, proj, short_taps)
    edge = permuted(edge, both, devices, -1)
    edge = jnp.where(at_end, jnp.zeros_like(edge), edge)
    input_half, own, other = mixer_back(
        grad01, third, edge, proj, n1, mid, own_rows, mixer_gain[None], w_in, short_taps, out_grad_w, gain_two, g1, g2
    )
    total = (own + swapped(other).astype(F32)).astype(BF)
    part = exchanged(total, "seq").reshape(seq_devices, -1, model + LANES)
    part = jnp.sum(part.astype(F32), axis=0).astype(BF)
    mine = gathered_all(part, seq_devices).reshape(2 * width, model + LANES)
    theirs = swapped(mine)
    first = jnp.where(tp_index == 0, mine, theirs).astype(F32)
    second = jnp.where(tp_index == 0, theirs, mine).astype(F32)
    big = jnp.concatenate([first, second], axis=0)[:, :model]
    small = first[:, model:]
    pieces = model // LANES
    vectors = small[: pieces * 16].reshape(pieces, 16, LANES).transpose(1, 0, 2).reshape(16, model)
    base = pieces * 16
    tail = small[base + hidden : base + hidden + 8]
    input_other = swapped(input_half)
    input_grad = jnp.where(
        tp_index == 0,
        jnp.concatenate([input_half, input_other], axis=0),
        jnp.concatenate([input_other, input_half], axis=0),
    )
    g3 = g3[:chans]
    g3_other = swapped(g3)
    g3_full = jnp.where(
        tp_index == 0, jnp.concatenate([g3, g3_other], axis=0), jnp.concatenate([g3_other, g3], axis=0)
    ).T
    return (
        layer_output,
        input_grad,
        vectors[9],
        big[: 3 * width].reshape(3, width, model).transpose(1, 0, 2),
        vectors[:9].reshape(3, 3, model).transpose(1, 0, 2),
        tail[:5],
        tail[5],
        small[base : base + hidden],
        g3_full,
        big[3 * width :],
        vectors[10],
        glu_all[:, :2].transpose(0, 2, 1, 3).astype(F32),
        glu_all[:, 2].transpose(2, 0, 1).reshape(half, model).astype(F32),
    )


def solution(mesh):
    placed = (
        P("seq", None),
        P(),
        P(),
        P(),
        P(),
        P(),
        P(),
        P(None, "seq"),
        P("seq"),
        P(),
        P(),
        P(None, None, None, "tp"),
        P("tp", None),
        P(("seq", "tp"), None),
    )
    return jax.shard_map(
        local,
        mesh=mesh,
        in_specs=placed,
        out_specs=(
            P(("seq", "tp"), None),
            P("seq", None),
            P(),
            P(),
            P(),
            P(),
            P(),
            P(),
            P(None, "seq"),
            P(),
            P(),
            P(None, None, None, "tp"),
            P("tp", None),
        ),
        check_vma=False,
    )
```

time: 538 us -> 257 us (0.48)
  matrix products: 189 us -> 0 us
  Pallas kernels: 0 us -> 74 us
  blocking collectives: 90.3 us -> 23.4 us
  local copies, waits for them, and re-layouts: 58.8 us -> 22.2 us
  waiting for transfers between devices: 115 us -> 79.4 us
  other arithmetic: 33.5 us -> 11 us
  between operations: 15.4 us -> 0.96 us
  starting transfers between devices: 28.2 us -> 41.5 us
    dot_general x56 -> x0, matrix products: 189 us -> none  [the longest x3 51.1 us: filter_taps(): jnp.dot(hidden_first, weight_second, precision=EXACT_PRODUCT)]
    psum x1 -> x0, waiting for transfers between devices: 95.9 us -> none  [local(): lax.psum((mixer_gain_grad, in_proj_grad, short_taps_grad, weight_first_gr...]
    psum x1 -> x0, blocking collectives: 81.6 us -> none  [local(): lax.psum((mixer_gain_grad, in_proj_grad, short_taps_grad, weight_first_gr...]
    pallas_call x0 -> x11, Pallas kernels: none -> 74 us  [the longest x1 16.5 us: filter_forward(): pl.pallas_call(functools.partial(filter_forward_kernel, seq_length), grid...]
    all_to_all x4 -> x8, waiting for transfers between devices: 9.67 us -> 76.5 us  [exchanged(): return lax.all_to_all(x, axes, 0, 0, axis_index_groups=groups, tiled=True)]
    all_to_all x0 -> x2, blocking collectives: none -> 23.4 us  [exchanged(): return lax.all_to_all(x, axes, 0, 0, axis_index_groups=groups, tiled=True)]
    unnamed x204 -> x37, local copies, waits for them, and re-layouts: 28.1 us -> 9.82 us
    reshape x7 -> x3, local copies, waits for them, and re-layouts: 13.9 us -> 1.22 us  [the longest x1 1.19 us: local(): down_own = glu_out.reshape(half, blocks, width).transpose(1, 0, 2)]
  transfers between devices with their start and end apart: 9 -> 17, of which waited for: 5 -> 9; matrix products, arithmetic and copies ran while one was open for 30% -> 8% of each run, Pallas kernels for 0% -> 21%
where the time goes in v1:
time: 257 us; the launch traced here: 253 us
  waiting for transfers between devices  79.4 us (31%)
  Pallas kernels  74 us (29%)
  starting transfers between devices  41.5 us (16%)
  blocking collectives  23.4 us (9%)
  local copies, waits for them, and re-layouts  22.2 us (9%)
  other arithmetic  11 us (4%)
    all_to_all x8, waiting for transfers between devices, exchanged(): return lax.all_to_all(x, axes, 0, 0, axis_index_groups=groups, tiled=True)  76.5 us
    all_to_all x8, starting transfers between devices, exchanged(): return lax.all_to_all(x, axes, 0, 0, axis_index_groups=groups, tiled=True)  33.1 us
    all_to_all x2, blocking collectives, exchanged(): return lax.all_to_all(x, axes, 0, 0, axis_index_groups=groups, tiled=True)  23.4 us
    pallas_call x1, Pallas kernels, filter_forward(): pl.pallas_call(functools.partial(filter_forward_kernel, seq_length), grid...  16.5 us
    pallas_call x1, Pallas kernels, filter_backward(): pl.pallas_call(functools.partial(filter_backward_kernel, seq_length), gri...  11.9 us
    pallas_call x2, Pallas kernels, conv_call(): pl.pallas_call(functools.partial(kernel, padded, seqs), in_specs=vmem_spe...  10.8 us
    unnamed x37, local copies, waits for them, and re-layouts  9.82 us
    pallas_call x1, Pallas kernels, middle_part(): pl.pallas_call(middle_kernel, in_specs=vmem_specs(10), out_specs=vmem_spe...  7.9 us
  transfers between devices with their start and end apart: 17, of which 9 were waited for; matrix products, arithmetic and copies ran while one was open for 8% of the time, Pallas kernels for 21%

profile of v1, /device:TPU:0, one launch (start us, length us, event | category | flops | bytes accessed | tf_op | source)
XLA Modules:
  0.0 252.6 jit_solution(11318199083726341796)
XLA Ops:
  0.7 1.0 copy-done
  1.6 2.3 collective-permute-start
  4.0 1.4 copy.49
  5.4 2.7 %collective-permute-start.2 = (bf16[4,384,192]{1,2,0:T(8,128)(2,1)S(1)}, bf16[4,384,192]{1,2,0:T(8,128)(2,1)}, u32[]{:S(2)}, u32[]{:S(2)}) collective-permute-start(bf16[4,384,192]{1,2,0:T(8,128)(2,1)S(1)} %bitcast.54), channel_id=1, source_target_pairs={{0,1},{1,0},{2,3},{3,2},{4,5},{5,4},{6,7},{7,6},{8,9},{9,8},{10,11... | collective-permute-start | bytes 1769480 | tf_op jit(solution)/shard_map/ppermute | solution.py:701
  8.4 0.8 maximum_maximum_fusion.w1_ref
  9.2 0.7 constant_dynamic-slice_fusion.1.x_ref
  9.9 0.6 broadcast_in_dim.38.gain_ref
  10.6 0.6 broadcast_select_fusion.1.halo_ref
  11.2 3.3 %mixer_in.1 = (bf16[768,128]{1,0:T(8,128)(2,1)}, bf16[128,768]{1,0:T(8,128)(2,1)}, bf16[3,144,768]{2,1,0:T(8,128)(2,1)}, f32[128,768]{1,0:T(8,128)}) custom-call(bf16[128,768]{1,0:T(8,128)(2,1)} %constant_dynamic-slice_fusion.1.x_ref, bf16[16,768]{1,0:T(8,128)(2,1)} %broadcast_select_fusion.1.halo_ref, f32[1,768]{1,0:T(1,128)} %broadcast_in_dim.38.gain_ref, ...), custom_call_target="tpu_custom_call" | custom-call | flops 3000000000 | bytes 4000000 | tf_op jit(solution)/shard_map/mixer_in/pallas_call | solution.py:452
  14.5 4.9 %all-to-all-start = ((bf16[32,24,128]{2,1,0:T(8,128)(2,1)}), bf16[32,24,128]{2,1,0:T(8,128)(2,1)S(1)}, u32[]{:S(2)}, u32[]{:S(2)}) async-start(bf16[32,24,128]{2,1,0:T(8,128)(2,1)} %bitcast.67), calls=%async_computation | async-start | bytes 393216 | tf_op jit(solution)/shard_map/all_to_all | solution.py:705
  19.5 0.6 dynamic-slice_bitcast_fusion.w3_ref
  20.1 0.7 broadcast_in_dim.41.decay_ref
  20.7 16.5 %filter_forward.1 = (f32[24,8192]{1,0:T(8,128)}, bf16[128,8192]{1,0:T(8,128)(2,1)}, bf16[128,8192]{1,0:T(8,128)(2,1)}, bf16[128,8192]{1,0:T(8,128)(2,1)}, bf16[128,8192]{1,0:T(8,128)(2,1)}) custom-call(bf16[48,8192]{1,0:T(8,128)(2,1)} %constant.66.clone.feat_ref, f32[8,128]{1,0:T(8,128)} %maximum_maximum_fusion.w1_ref, f32[128,128]{1,0:T(8,128)} %w2_ref.3, ...), custom_call_target="tpu_custom_call" | custom-call | flops 1056964608 | bytes 8388608 | tf_op jit(solution)/shard_map/filter_forward/pallas_call | solution.py:183
  37.2 4.3 %filter_spectrum.1.h_ref = f32[960,256]{1,0:T(8,128)} custom-call(f32[24,8192]{1,0:T(8,128)} %get-tuple-element.44.lag_ref, bf16[640,512]{1,0:T(8,128)(2,1)} %constant.67.clone.fh, bf16[640,512]{1,0:T(8,128)(2,1)} %constant.68.clone.fl, f32[4,40,128]{2,1,0:T(8,128)} %constant.69.clone.tw, bf16[256,256]{1,0:T(8,128)(2,1)} %constant.70.clone.sh, ...), custom_call_target="tpu_custom_call" | custom-call | flops 2000000000 | bytes 4000000 | tf_op jit(solution)/shard_map/filter_spectrum/pallas_call | solution.py:358
  41.5 0.7 copy-done.7
  42.2 5.4 %conv_forward.1 = (bf16[32,24,128]{2,1,0:T(8,128)(2,1)}, f32[960,256]{1,0:T(8,128)}) custom-call(bf16[32,24,128]{2,1,0:T(8,128)(2,1)} %copy-done.7, f32[960,256]{1,0:T(8,128)} %filter_spectrum.1.h_ref, bf16[640,512]{1,0:T(8,128)(2,1)} %constant.67.clone.fh, bf16[640,512]{1,0:T(8,128)(2,1)} %constant.68.clone.fl, f32[4,40,128]{2,1,0:T(8,128)} %constant.69.clone.tw, ...), custom_call_target="tpu_custom_call" | custom-call | flops 4000000000 | bytes 6000000 | tf_op jit(solution)/shard_map/conv_forward/pallas_call | solution.py:372
  47.6 5.8 %all-to-all-start.1 = ((bf16[32,24,128]{2,1,0:T(8,128)(2,1)}), bf16[32,24,128]{2,1,0:T(8,128)(2,1)S(1)}, u32[]{:S(2)}, u32[]{:S(2)}) async-start(bf16[32,24,128]{2,1,0:T(8,128)(2,1)} %get-tuple-element.45), calls=%async_computation.1 | async-start | bytes 393216 | tf_op jit(solution)/shard_map/all_to_all | solution.py:705
  53.4 0.6 broadcast_in_dim.42.gain_ref
  54.0 1.2 copy.50
  55.2 2.2 copy.52.db_ref
  57.4 4.9 %all-to-all-done.1 = bf16[32,24,128]{2,1,0:T(8,128)(2,1)S(1)} async-done(((bf16[32,24,128]{2,1,0:T(8,128)(2,1)}), bf16[32,24,128]{2,1,0:T(8,128)(2,1)S(1)}, u32[]{:S(2)}, u32[]{:S(2)}) %all-to-all-start.1) | async-done | bytes 196640 | tf_op jit(solution)/shard_map/all_to_all | solution.py:705
  62.3 0.7 copy-done.5
  63.0 7.9 %middle_part.1 = (bf16[768,128]{1,0:T(8,128)(2,1)}, f32[128,768]{1,0:T(8,128)}, f32[128,768]{1,0:T(8,128)}, bf16[128,768]{1,0:T(8,128)(2,1)}, bf16[768,128]{1,0:...) custom-call(bf16[768,128]{1,0:T(8,128)(2,1)} %bitcast.66, f32[128,768]{1,0:T(8,128)} %get-tuple-element.46.sm2_ref, ...), custom_call_target="tpu_custom_call" | custom-call | flops 8999999488 | bytes 6000000 | tf_op jit(solution)/shard_map/middle_part/pallas_call | solution.py:534
  70.9 12.3 %all_to_all.54.x_ref = bf16[32,24,128]{2,1,0:T(8,128)(2,1)} all-to-all(bf16[32,24,128]{2,1,0:T(8,128)(2,1)} %bitcast.68), channel_id=1, replica_groups=mesh['seq'=16,'tp'=2] {'seq','tp'}, dimensions={0} | all-to-all | bytes 393216 | tf_op jit(solution)/shard_map/all_to_all | solution.py:705
  83.2 5.4 %conv_backward.1 = (bf16[32,24,128]{2,1,0:T(8,128)(2,1)}, f32[960,256]{1,0:T(8,128)}) custom-call(bf16[32,24,128]{2,1,0:T(8,128)(2,1)} %all_to_all.54.x_ref, f32[960,256]{1,0:T(8,128)} %filter_spectrum.1.h_ref, bf16[640,512]{1,0:T(8,128)(2,1)} %constant.67.clone.fh, bf16[640,512]{1,0:T(8,128)(2,1)} %constant.68.clone.fl, f32[4,40,128]{2,1,0:T(8,128)} %constant.69.clone.tw, ...), custom_call_target="tpu_custom_call" | custom-call | flops 4000000000 | bytes 6000000 | tf_op jit(solution)/shard_map/conv_backward/pallas_call | solution.py:372
  88.6 2.6 %all-to-all-start.3 = ((bf16[32,24,128]{2,1,0:T(8,128)(2,1)}), bf16[32,24,128]{2,1,0:T(8,128)(2,1)S(1)}, u32[]{:S(2)}, u32[]{:S(2)}) async-start(bf16[32,24,128]{2,1,0:T(8,128)(2,1)} %get-tuple-element.49), calls=%async_computation.3 | async-start | bytes 393216 | tf_op jit(solution)/shard_map/all_to_all | solution.py:705
  91.3 5.3 %filter_grad.1.grad_ref = f32[24,8192]{1,0:T(8,128)} custom-call(f32[960,256]{1,0:T(8,128)} %get-tuple-element.58.spec_ref, f32[960,256]{1,0:T(8,128)} %get-tuple-element.59.saved_ref, f32[4,40,128]{2,1,0:T(8,128)} %constant.69.clone.tw, bf16[256,256]{1,0:T(8,128)(2,1)} %constant.72.clone.ih, bf16[256,256]{1,0:T(8,128)(2,1)} %constant.73.clone.il, ...), custom_call_target="tpu_custom_call" | custom-call | flops 3000000000 | bytes 6000000 | tf_op jit(solution)/shard_map/filter_grad/pallas_call | solution.py:388
  96.5 3.6 %all-to-all-done.3 = bf16[32,24,128]{2,1,0:T(8,128)(2,1)S(1)} async-done(((bf16[32,24,128]{2,1,0:T(8,128)(2,1)}), bf16[32,24,128]{2,1,0:T(8,128)(2,1)S(1)}, u32[]{:S(2)}, u32[]{:S(2)}) %all-to-all-start.3) | async-done | bytes 196640 | tf_op jit(solution)/shard_map/all_to_all | solution.py:705
  100.1 0.7 copy-done.4
  100.8 2.6 %short_grads.1 = (f32[2,128,768]{2,1,0:T(8,128)}, f32[3,8,768]{2,1,0:T(8,128)}) custom-call(bf16[768,128]{1,0:T(8,128)(2,1)} %bitcast.65, f32[128,768]{1,0:T(8,128)} %get-tuple-element.50.third_ref, bf16[3,144,768]{2,1,0:T(8,128)(2,1)} %get-tuple-element.51.proj_ref, f32[3,3,768]{2,1,0:T(4,128)} %taps_ref.5), custom_call_target="tpu_custom_call" | custom-call | flops 1000000000 | bytes 2000000 | tf_op jit(solution)/shard_map/short_grads/pallas_call | solution.py:618
  103.4 1.3 collective-permute-start.3
  104.7 11.9 %filter_backward.1 = (f32[8,128]{1,0:T(8,128)}, f32[128,128]{1,0:T(8,128)}, f32[24,128]{1,0:T(8,128)}) custom-call(f32[24,8192]{1,0:T(8,128)} %filter_grad.1.grad_ref, bf16[48,8192]{1,0:T(8,128)(2,1)} %constant.66.clone.feat_ref, f32[128,128]{1,0:T(8,128)} %w2_ref.3, f32[24,128]{1,0:T(8,128)} %dynamic-slice_bitcast_fusion.w3_ref, ...), custom_call_target="tpu_custom_call" | custom-call | flops 1761607680 | bytes 8388608 | tf_op jit(solution)/shard_map/filter_backward/pallas_call | solution.py:227
  116.6 0.6 broadcast_select_fusion.halo_ref
  117.2 5.7 %mixer_back.1 = (bf16[128,768]{1,0:T(8,128)(2,1)}, f32[384,896]{1,0:T(8,128)}, bf16[384,896]{1,0:T(8,128)(2,1)}) custom-call(f32[2,128,768]{2,1,0:T(8,128)} %get-tuple-element.52.grad_ref, f32[128,768]{1,0:T(8,128)} %get-tuple-element.50.third_ref, f32[3,8,768]{2,1,0:T(8,128)} %broadcast_select_fusion.halo_ref, ...), custom_call_target="tpu_custom_call" | custom-call | flops 4000000000 | bytes 6000000 | tf_op jit(solution)/shard_map/mixer_back/pallas_call | solution.py:679
  122.9 1.2 collective-permute-start.5
  124.3 11.1 %all_to_all.55.og_ref = bf16[4,192,128]{2,1,0:T(8,128)(2,1)} all-to-all(bf16[4,192,128]{2,1,0:T(8,128)(2,1)S(1)} %bitcast.60), channel_id=1, replica_groups={{0,8,16,24},{2,10,18,26},{4,12,20,28},{6,14,22,30},{1,9,17,25},{3,11,19..., dimensions={0} | all-to-all | bytes 393216 | tf_op jit(solution)/shard_map/all_to_all | solution.py:705
  135.4 3.4 %all-to-all-start.6 = ((bf16[4,192,128]{2,1,0:T(8,128)(2,1)}), bf16[4,192,128]{2,1,0:T(8,128)(2,1)S(1)}, u32[]{:S(2)}, u32[]{:S(2)}) async-start(bf16[4,192,128]{2,1,0:T(8,128)(2,1)} %bitcast.22), calls=%async_computation.6 | async-start | bytes 393216 | tf_op jit(solution)/shard_map/all_to_all | solution.py:705
  138.8 2.3 add_convert_fusion
  141.1 4.8 %all-to-all-done.6.x_ref = bf16[4,192,128]{2,1,0:T(8,128)(2,1)S(1)} async-done(((bf16[4,192,128]{2,1,0:T(8,128)(2,1)}), bf16[4,192,128]{2,1,0:T(8,128)(2,1)S(1)}, u32[]{:S(2)}, u32[]{:S(2)}) %all-to-all-start.6) | async-done | bytes 196640 | tf_op jit(solution)/shard_map/all_to_all | solution.py:705
  145.9 4.1 %all-to-all-start.4 = ((bf16[16,24,896]{2,1,0:T(8,128)(2,1)}), bf16[16,24,896]{2,1,0:T(8,128)(2,1)S(1)}, u32[]{:S(2)}, u32[]{:S(2)}) async-start(bf16[16,24,896]{2,1,0:T(8,128)(2,1)} %bitcast.11), calls=%async_computation.4 | async-start | bytes 1376256 | tf_op jit(solution)/shard_map/all_to_all | solution.py:705
  150.0 5.9 %glu_grads.1 = (f32[576,384]{1,0:T(8,128)}, bf16[576,384]{1,0:T(8,128)(2,1)}) custom-call(bf16[4,192,128]{2,1,0:T(8,128)(2,1)} %copy-done.6, bf16[4,192,128]{2,1,0:T(8,128)(2,1)} %all_to_all.55.og_ref, bf16[4,2,192,384]{3,2,1,0:T(8,128)(2,1)} %bitcast.59, bf16[4,2,192,384]{3,2,1,0:T(8,128)(2,1)} %collective-permute-done.1.gb_ref, ...), custom_call_target="tpu_custom_call" | custom-call | flops 8999999488 | bytes 4000000 | tf_op jit(solution)/shard_map/glu_grads/pallas_call | solution.py:580
  155.9 2.0 collective-permute-done.8
  157.9 2.0 add_convert_fusion.1
  159.9 7.2 %all-to-all-done.4 = bf16[16,24,896]{2,1,0:T(8,128)(2,1)S(1)} async-done(((bf16[16,24,896]{2,1,0:T(8,128)(2,1)}), bf16[16,24,896]{2,1,0:T(8,128)(2,1)S(1)}, u32[]{:S(2)}, u32[]{:S(2)}) %all-to-all-start.4) | async-done | bytes 688160 | tf_op jit(solution)/shard_map/all_to_all | solution.py:705
  167.1 3.5 %all-to-all-start.8 = ((bf16[4,144,384]{2,1,0:T(8,128)(2,1)}), bf16[4,144,384]{2,1,0:T(8,128)(2,1)S(1)}, u32[]{:S(2)}, u32[]{:S(2)}) async-start(bf16[4,144,384]{2,1,0:T(8,128)(2,1)} %bitcast.25), calls=%async_computation.8 | async-start | bytes 884736 | tf_op jit(solution)/shard_map/all_to_all | solution.py:705
  170.7 6.0 %all-to-all-done.8 = bf16[4,144,384]{2,1,0:T(8,128)(2,1)S(1)} async-done(((bf16[4,144,384]{2,1,0:T(8,128)(2,1)}), bf16[4,144,384]{2,1,0:T(8,128)(2,1)S(1)}, u32[]{:S(2)}, u32[]{:S(2)}) %all-to-all-start.8) | async-done | bytes 442400 | tf_op jit(solution)/shard_map/all_to_all | solution.py:705
  176.7 0.9 broadcast_in_dim.44
  177.6 4.4 %all-to-all-start.5 = ((bf16[16,24,896]{2,1,0:T(8,128)(2,1)}), bf16[16,24,896]{2,1,0:T(8,128)(2,1)}, u32[]{:S(2)}, u32[]{:S(2)}) async-start(bf16[16,24,896]{2,1,0:T(8,128)(2,1)} %broadcast_in_dim.44), calls=%async_computation.5 | async-start | bytes 1376256 | tf_op jit(solution)/shard_map/all_to_all | solution.py:705
  182.1 16.7 %all-to-all-done.5 = bf16[16,24,896]{2,1,0:T(8,128)(2,1)} async-done(((bf16[16,24,896]{2,1,0:T(8,128)(2,1)}), bf16[16,24,896]{2,1,0:T(8,128)(2,1)}, u32[]{:S(2)}, u32[]{:S(2)}) %all-to-all-start.5) | async-done | bytes 688160 | tf_op jit(solution)/shard_map/all_to_all | solution.py:705
  198.8 1.4 broadcast_in_dim.45
  200.2 4.4 %all-to-all-start.9 = ((bf16[16,144,384]{2,1,0:T(8,128)(2,1)}), bf16[16,144,384]{2,1,0:T(8,128)(2,1)S(1)}, u32[]{:S(2)}, u32[]{:S(2)}) async-start(bf16[16,144,384]{2,1,0:T(8,128)(2,1)} %broadcast_in_dim.45), calls=%async_computation.9 | async-start | bytes 3538944 | tf_op jit(solution)/shard_map/all_to_all | solution.py:705
  205.1 0.9 collective-permute-done.7
  206.1 0.6 fusion.1
  206.9 0.8 maximum_select_fusion
  207.8 33.3 %all-to-all-done.9 = bf16[16,144,384]{2,1,0:T(8,128)(2,1)S(1)} async-done(((bf16[16,144,384]{2,1,0:T(8,128)(2,1)}), bf16[16,144,384]{2,1,0:T(8,128)(2,1)S(1)}, u32[]{:S(2)}, u32[]{:S(2)}) %all-to-all-start.9) | async-done | bytes 1769504 | tf_op jit(solution)/shard_map/all_to_all | solution.py:705
  241.1 1.4 copy.58
  242.7 3.2 %copy.57 = f32[4,192,2,384]{3,2,1,0:T(2,128)} copy(f32[4,192,2,384]{3,1,2,0:T(8,128)S(1)} %convert_bitcast_fusion) | data formatting | bytes 4718592
  245.9 1.5 select_convert_fusion
  247.9 0.6 slice.65
  248.5 0.6 slice_bitcast_fusion.1
  249.1 0.6 slice.67
  249.8 1.3 pad_maximum_fusion
  251.1 0.9 slice.68
  252.0 0.6 copy.56
  (56 shorter events, 2.4 us)
Async XLA Ops:
  0.6 1.0 copy-start
  0.7 7.4 %copy-start.1 = (bf16[4,192,2,384]{3,2,1,0:T(2,128)(2,1)S(1)}, bf16[4,192,2,384]{3,2,1,0:T(2,128)(2,1)}, u32[]{:S(2)}) copy-start(bf16[4,192,2,384]{3,2,1,0:T(2,128)(2,1)} %param.35) | copy-start | bytes 3538948
  1.6 9.0 %collective-permute-start = (bf16[16,768]{1,0:T(8,128)(2,1)S(1)}, bf16[16,768]{1,0:T(8,128)(2,1)S(1)}, u32[]{:S(2)}, u32[]{:S(2)}) collective-permute-start(bf16[16,768]{1,0:T(8,128)(2,1)S(1)} %constant_dynamic-slice_fusion), channel_id=1, source_target_pairs={{0,1},{1,2},{2,3},{3,4},{4,5},{5,6},{6,7},{7,8},{8,9},{9,10},{10,1... | collective-permute-start | bytes 73736 | tf_op jit(solution)/shard_map/ppermute | solution.py:697
  5.4 3.1 %copy-start.13 = (f32[5,128]{1,0:T(8,128)S(1)}, f32[5,128]{1,0:T(8,128)}, u32[]{:S(2)}) copy-start(f32[5,128]{1,0:T(8,128)} %param.28) | copy-start | bytes 7684
  5.4 3.1 %copy-start.14 = (f32[128]{0:T(128)S(1)}, f32[128]{0:T(128)}, u32[]{:S(2)}) copy-start(f32[128]{0:T(128)} %param.29) | copy-start | bytes 1540
  5.4 4.5 %copy-start.11 = (f32[768]{0:T(1024)S(1)}, f32[768]{0:T(1024)}, u32[]{:S(2)}) copy-start(f32[768]{0:T(1024)} %param.25) | copy-start | bytes 9220
  5.4 5.1 %copy-start.15 = (f32[48]{0:T(128)S(1)}, f32[48]{0:T(128)}, u32[]{:S(2)}) copy-start(f32[48]{0:T(128)} %param.32) | copy-start | bytes 580
  5.4 49.8 %collective-permute-start.2 = (bf16[4,384,192]{1,2,0:T(8,128)(2,1)S(1)}, bf16[4,384,192]{1,2,0:T(8,128)(2,1)}, u32[]{:S(2)}, u32[]{:S(2)}) collective-permute-start(bf16[4,384,192]{1,2,0:T(8,128)(2,1)S(1)} %bitcast.54), channel_id=1, source_target_pairs={{0,1},{1,0},{2,3},{3,2},{4,5},{5,4},{6,7},{7,6},{8,9},{9,8},{10,11... | collective-permute-start | bytes 1769480 | tf_op jit(solution)/shard_map/ppermute | solution.py:701
  8.3 6.3 %copy-start.2 = (bf16[4,192,2,384]{3,1,2,0:T(8,128)(2,1)}, bf16[4,192,2,384]{3,1,2,0:T(8,128)(2,1)S(1)}, u32[]{:S(2)}) copy-start(bf16[4,192,2,384]{3,1,2,0:T(8,128)(2,1)S(1)} %copy.63) | copy-start | bytes 3538948
  8.3 54.0 %collective-permute-start.1 = (bf16[4,2,192,384]{3,2,1,0:T(8,128)(2,1)S(1)}, bf16[4,2,192,384]{3,2,1,0:T(8,128)(2,1)}, u32[]{:S(2)}, u32[]{:S(2)}) collective-permute-start(bf16[4,2,192,384]{3,2,1,0:T(8,128)(2,1)S(1)} %bitcast.57), channel_id=1, source_target_pairs={{0,1},{1,0},{2,3},{3,2},{4,5},{5,4},{6,7},{7,6},{8,9},{9,8},{10,11... | collective-permute-start | bytes 3538952 | tf_op jit(solution)/shard_map/ppermute | solution.py:701
  11.2 8.2 %copy-start.10 = (f32[128,48]{0,1:T(8,128)S(1)}, f32[128,48]{0,1:T(8,128)}, u32[]{:S(2)}) copy-start(f32[128,48]{0,1:T(8,128)} %param.31) | copy-start | bytes 73732
  14.5 27.0 %all-to-all-start = ((bf16[32,24,128]{2,1,0:T(8,128)(2,1)}), bf16[32,24,128]{2,1,0:T(8,128)(2,1)S(1)}, u32[]{:S(2)}, u32[]{:S(2)}) async-start(bf16[32,24,128]{2,1,0:T(8,128)(2,1)} %bitcast.67), calls=%async_computation | async-start | bytes 393216 | tf_op jit(solution)/shard_map/all_to_all | solution.py:705
  41.5 11.9 %copy-start.12 = (f32[768]{0:T(1024)S(1)}, f32[768]{0:T(1024)}, u32[]{:S(2)}) copy-start(f32[768]{0:T(1024)} %param.34) | copy-start | bytes 9220
  41.5 0.7 copy-start.7
  47.6 14.7 %all-to-all-start.1 = ((bf16[32,24,128]{2,1,0:T(8,128)(2,1)}), bf16[32,24,128]{2,1,0:T(8,128)(2,1)S(1)}, u32[]{:S(2)}, u32[]{:S(2)}) async-start(bf16[32,24,128]{2,1,0:T(8,128)(2,1)} %get-tuple-element.45), calls=%async_computation.1 | async-start | bytes 393216 | tf_op jit(solution)/shard_map/all_to_all | solution.py:705
  62.3 0.7 copy-start.5
  88.6 11.5 %all-to-all-start.3 = ((bf16[32,24,128]{2,1,0:T(8,128)(2,1)}), bf16[32,24,128]{2,1,0:T(8,128)(2,1)S(1)}, u32[]{:S(2)}, u32[]{:S(2)}) async-start(bf16[32,24,128]{2,1,0:T(8,128)(2,1)} %get-tuple-element.49), calls=%async_computation.3 | async-start | bytes 393216 | tf_op jit(solution)/shard_map/all_to_all | solution.py:705
  100.1 0.7 copy-start.4
  103.4 13.2 %collective-permute-start.3 = (f32[3,8,768]{2,1,0:T(8,128)}, f32[3,8,768]{2,1,0:T(8,128)S(1)}, u32[]{:S(2)}, u32[]{:S(2)}) collective-permute-start(f32[3,8,768]{2,1,0:T(8,128)} %get-tuple-element.53), channel_id=1, source_target_pairs={{1,0},{2,1},{3,2},{4,3},{5,4},{6,5},{7,6},{8,7},{9,8},{10,9},{11,1... | collective-permute-start | bytes 221192 | tf_op jit(solution)/shard_map/ppermute | solution.py:697
  117.2 6.9 %copy-start.3 = (bf16[128,768]{1,0:T(8,128)(2,1)S(1)}, bf16[128,768]{1,0:T(8,128)(2,1)}, u32[]{:S(2)}) copy-start(bf16[128,768]{1,0:T(8,128)(2,1)} %og_ref.1) | copy-start | bytes 589828
  122.9 15.9 %collective-permute-start.5 = (bf16[384,896]{1,0:T(8,128)(2,1)}, bf16[384,896]{1,0:T(8,128)(2,1)S(1)}, u32[]{:S(2)}, u32[]{:S(2)}) collective-permute-start(bf16[384,896]{1,0:T(8,128)(2,1)} %get-tuple-element.68), channel_id=1, source_target_pairs={{0,1},{1,0},{2,3},{3,2},{4,5},{5,4},{6,7},{7,6},{8,9},{9,8},{10,11... | collective-permute-start | bytes 2064392 | tf_op jit(solution)/shard_map/ppermute | solution.py:701
  135.4 10.5 %all-to-all-start.6 = ((bf16[4,192,128]{2,1,0:T(8,128)(2,1)}), bf16[4,192,128]{2,1,0:T(8,128)(2,1)S(1)}, u32[]{:S(2)}, u32[]{:S(2)}) async-start(bf16[4,192,128]{2,1,0:T(8,128)(2,1)} %bitcast.22), calls=%async_computation.6 | async-start | bytes 393216 | tf_op jit(solution)/shard_map/all_to_all | solution.py:705
  145.9 4.1 %copy-start.6 = (bf16[4,192,128]{2,1,0:T(8,128)(2,1)}, bf16[4,192,128]{2,1,0:T(8,128)(2,1)S(1)}, u32[]{:S(2)}) copy-start(bf16[4,192,128]{2,1,0:T(8,128)(2,1)S(1)} %all-to-all-done.6.x_ref) | copy-start | bytes 589828
  145.9 21.2 %all-to-all-start.4 = ((bf16[16,24,896]{2,1,0:T(8,128)(2,1)}), bf16[16,24,896]{2,1,0:T(8,128)(2,1)S(1)}, u32[]{:S(2)}, u32[]{:S(2)}) async-start(bf16[16,24,896]{2,1,0:T(8,128)(2,1)} %bitcast.11), calls=%async_computation.4 | async-start | bytes 1376256 | tf_op jit(solution)/shard_map/all_to_all | solution.py:705
  155.9 2.0 collective-permute-start.8
  167.1 9.6 %all-to-all-start.8 = ((bf16[4,144,384]{2,1,0:T(8,128)(2,1)}), bf16[4,144,384]{2,1,0:T(8,128)(2,1)S(1)}, u32[]{:S(2)}, u32[]{:S(2)}) async-start(bf16[4,144,384]{2,1,0:T(8,128)(2,1)} %bitcast.25), calls=%async_computation.8 | async-start | bytes 884736 | tf_op jit(solution)/shard_map/all_to_all | solution.py:705
  177.6 21.2 %all-to-all-start.5 = ((bf16[16,24,896]{2,1,0:T(8,128)(2,1)}), bf16[16,24,896]{2,1,0:T(8,128)(2,1)}, u32[]{:S(2)}, u32[]{:S(2)}) async-start(bf16[16,24,896]{2,1,0:T(8,128)(2,1)} %broadcast_in_dim.44), calls=%async_computation.5 | async-start | bytes 1376256 | tf_op jit(solution)/shard_map/all_to_all | solution.py:705
  200.2 4.4 %copy-start.8 = (bf16[128,768]{1,0:T(8,128)(2,1)S(1)}, bf16[128,768]{1,0:T(8,128)(2,1)}, u32[]{:S(2)}) copy-start(bf16[128,768]{1,0:T(8,128)(2,1)} %get-tuple-element.66) | copy-start | bytes 589828
  200.2 4.5 %copy-start.9 = (f32[24,128]{1,0:T(8,128)S(1)}, f32[24,128]{1,0:T(8,128)}, u32[]{:S(2)}) copy-start(f32[24,128]{1,0:T(8,128)} %get-tuple-element.69) | copy-start | bytes 36868
  200.2 40.8 %all-to-all-start.9 = ((bf16[16,144,384]{2,1,0:T(8,128)(2,1)}), bf16[16,144,384]{2,1,0:T(8,128)(2,1)S(1)}, u32[]{:S(2)}, u32[]{:S(2)}) async-start(bf16[16,144,384]{2,1,0:T(8,128)(2,1)} %broadcast_in_dim.45), calls=%async_computation.9 | async-start | bytes 3538944 | tf_op jit(solution)/shard_map/all_to_all | solution.py:705
  204.6 2.4 collective-permute-start.4
  204.7 1.4 collective-permute-start.7
  206.7 39.2 %collective-permute-start.6 = (bf16[384,896]{1,0:T(8,128)(2,1)}, bf16[384,896]{1,0:T(8,128)(2,1)}, u32[]{:S(2)}, u32[]{:S(2)}) collective-permute-start(bf16[384,896]{1,0:T(8,128)(2,1)} %bitcast.12), channel_id=1, source_target_pairs={{0,1},{1,0},{2,3},{3,2},{4,5},{5,4},{6,7},{7,6},{8,9},{9,8},{10,11... | collective-permute-start | bytes 2064392 | tf_op jit(solution)/shard_map/ppermute | solution.py:701
